TPU v7x, 32 devices: a whole 2x2x4 slice. The times are simulated.
32 devices in a mesh: batch: 8 (over z, x), chan: 4 (over y, core).
Axes of the slice: x: 2, y: 2, z: 4, core: 2. Of those that a mesh axis runs over, the one named last changes fastest.
Arguments:
- block_input: bfloat16 [128, 14, 14, 1024], P('batch', None, None, 'chan'), may hold values from -6 to 6
- first_reduce: float32 [1024, 512], P('batch', 'chan'), may hold values from -0.1875 to 0.1875
- first_spatial: float32 [3, 3, 512, 512], P(None, None, 'batch', 'chan'), may hold values from -0.09375 to 0.09375
- first_expand: float32 [512, 2048], P('chan', 'batch'), may hold values from -0.25 to 0.25
- first_shortcut: float32 [1024, 2048], P('batch', 'chan'), may hold values from -0.1875 to 0.1875
- second_reduce: float32 [2048, 512], P('batch', 'chan'), may hold values from -0.125 to 0.125
- second_spatial: float32 [3, 3, 512, 512], P(None, None, 'batch', 'chan'), may hold values from -0.09375 to 0.09375
- second_expand: float32 [512, 2048], P('chan', 'batch'), may hold values from -0.25 to 0.25
- first_mid_gain: float32 [2, 512], P(None, 'chan'), may hold values from 0.5 to 1.5
- first_mid_bias: float32 [2, 512], P(None, 'chan'), may hold values from -2.5 to 2.5
- first_wide_gain: float32 [2, 2048], P(None, 'chan'), may hold values from 0.5 to 1.5
- first_wide_bias: float32 [2, 2048], P(None, 'chan'), may hold values from -2.5 to 2.5
- second_mid_gain: float32 [2, 512], P(None, 'chan'), may hold values from 0.5 to 1.5
- second_mid_bias: float32 [2, 512], P(None, 'chan'), may hold values from -2.5 to 2.5
- second_wide_gain: float32 [2048], P('chan'), may hold values from 0.5 to 1.5
- second_wide_bias: float32 [2048], P('chan'), may hold values from -2.5 to 2.5
- subnet_widths: int32 [3], replicated, may hold values from 256 to 480, as said below
- subnet_ids: int32 [128], replicated, may hold values from 0 to 2, as said below
- crop_sides: int32 [128], replicated, may hold values from 2 to 14, as said below
- cotangent: bfloat16 [128, 7, 7, 2048], P('batch', None, None, 'chan'), may hold values from -6 to 6
Outputs:
- output: float32 [128, 7, 7, 2048], P('batch', None, None, 'chan')
- input_grad: float32 [128, 14, 14, 1024], P('batch', None, None, 'chan')
- first_reduce_grad: float32 [1024, 512], P('batch', 'chan')
- first_spatial_grad: float32 [3, 3, 512, 512], P(None, None, 'batch', 'chan')
- first_expand_grad: float32 [512, 2048], P('chan', 'batch')
- first_shortcut_grad: float32 [1024, 2048], P('batch', 'chan')
- second_reduce_grad: float32 [2048, 512], P('batch', 'chan')
- second_spatial_grad: float32 [3, 3, 512, 512], P(None, None, 'batch', 'chan')
- second_expand_grad: float32 [512, 2048], P('chan', 'batch')
- first_mid_gain_grad: float32 [2, 512], P(None, 'chan')
- first_mid_bias_grad: float32 [2, 512], P(None, 'chan')
- first_wide_gain_grad: float32 [2, 2048], P(None, 'chan')
- first_wide_bias_grad: float32 [2, 2048], P(None, 'chan')
- second_mid_gain_grad: float32 [2, 512], P(None, 'chan')
- second_mid_bias_grad: float32 [2, 512], P(None, 'chan')
- second_wide_gain_grad: float32 [2048], P('chan')
- second_wide_bias_grad: float32 [2048], P('chan')
Inputs may be any that keep to these rules, and one draw needn't show every extreme that they name: `subnet_widths`: multiples of 32; the smallest student has 256 channels and the largest 512 - 512 // 16. `subnet_ids`: every subnet trains at least one crop. `crop_sides`: even; crops 8k and 8k + 1 (an image's two large crops) have 14 - 2 or 14, the six others at most 6.
All inputs are finite; a program needn't handle non-finite values.
Results may differ from a plain program's by a relative error of at most 0.025.
Values may be sent and summed in bfloat16 or wider, within the bound.
No kernel may reach another device: no remote copies, remote signals or barrier semaphores. Data moves between devices by JAX's collectives and lax.ppermute only.
A program may use at most 192 MiB of HBM per device.

v0:
```python
import jax
import jax.numpy as jnp
from jax import lax
from jax.sharding import PartitionSpec as P

epsilon = 1e-05
precise = lax.Precision.HIGHEST


def silu_slope(values):
    sigmoid_val = jax.nn.sigmoid(values)
    return sigmoid_val * (1.0 + values * (1.0 - sigmoid_val))


def matmul_last(values, weight):
    return jnp.dot(values, weight, preferred_element_type=jnp.float32)


def matmul_back(upstream, weight):
    return jnp.einsum("chwm,km->chwk", upstream, weight, preferred_element_type=jnp.float32)


def matmul_back_t(upstream, weight):
    return jnp.einsum("chwm,mk->chwk", upstream, weight, preferred_element_type=jnp.float32)


def weight_term(values, upstream):
    return jnp.einsum("chwk,chwm->km", values, upstream, preferred_element_type=jnp.float32)


def rows_by_owner(weight, parts):
    share = weight.shape[0] // parts
    return weight.reshape(parts, share, weight.shape[1]).transpose(0, 2, 1)


def spatial_columns(activity, stride):
    padded = jnp.pad(activity, ((0, 0), (1, 1), (1, 1), (0, 0)))
    out_extent = activity.shape[1] // stride
    reach_span = stride * (out_extent - 1) + 1
    portions = [
        padded[
            :,
            offset_row : offset_row + reach_span : stride,
            offset_col : offset_col + reach_span : stride,
            :,
        ]
        for offset_row in range(3)
        for offset_col in range(3)
    ]
    return jnp.concatenate(portions, axis=3)


def spatial_scatter(columns, extent, stride):
    channels = columns.shape[3] // 9
    reach_span = stride * (columns.shape[1] - 1) + 1
    accumulated = jnp.zeros((columns.shape[0], extent + 2, extent + 2, channels), jnp.float32)
    for kernel_tap in range(9):
        offset_row, offset_col = divmod(kernel_tap, 3)
        portion = columns[..., kernel_tap * channels : (kernel_tap + 1) * channels]
        accumulated = accumulated + lax.pad(
            portion,
            jnp.float32(0.0),
            (
                (0, 0, 0),
                (offset_row, extent + 2 - offset_row - reach_span, stride - 1),
                (offset_col, extent + 2 - offset_col - reach_span, stride - 1),
                (0, 0, 0),
            ),
        )
    return accumulated[:, 1:-1, 1:-1, :]


def norm_forward(values, pixel_mask, member, counts, scaling, offset):
    masked = values * pixel_mask[..., None]
    first_local = jnp.dot(member, jnp.sum(masked, axis=(1, 2)), precision=precise)
    second_local = jnp.dot(member, jnp.sum(masked * values, axis=(1, 2)), precision=precise)
    first_total, second_total = lax.psum((first_local, second_local), "batch")
    average = first_total / counts[:, None]
    squares = second_total / counts[:, None]
    inverse = lax.rsqrt(squares - average * average + epsilon)
    crop_average = jnp.dot(member.T, average, precision=precise)
    crop_inverse = jnp.dot(member.T, inverse, precision=precise)
    centred = (values - crop_average[:, None, None, :]) * crop_inverse[:, None, None, :]
    return (scaling * centred + offset, centred, crop_inverse)


def norm_backward(upstream, centred, crop_inverse, pixel_mask, member, counts, scaling):
    bias_local = jnp.dot(member, jnp.sum(upstream, axis=(1, 2)), precision=precise)
    gain_local = jnp.dot(member, jnp.sum(upstream * centred, axis=(1, 2)), precision=precise)
    bias_total, gain_total = lax.psum((bias_local, gain_local), "batch")
    crop_bias = jnp.dot(member.T, bias_total / counts[:, None], precision=precise)
    crop_gain = jnp.dot(member.T, gain_total / counts[:, None], precision=precise)
    correction = pixel_mask[..., None] * (
        crop_bias[:, None, None, :] + centred * crop_gain[:, None, None, :]
    )
    result = scaling * crop_inverse[:, None, None, :] * (upstream - correction)
    return (result, jnp.sum(gain_total, axis=0), jnp.sum(bias_total, axis=0))


def gather_features(values):
    return lax.all_gather(values, "chan", axis=3, tiled=True)


def gather_mids(values):
    return lax.all_gather(values, "chan", axis=3, tiled=True)


def gather_wide(values):
    return lax.all_gather(values, "chan", axis=3, tiled=True)


def expand_channels(activity, columns_weight):
    whole_activity = lax.all_gather(activity, "chan", axis=3, tiled=True)
    result = matmul_last(whole_activity, columns_weight)
    return result


def spatial_back(grad_low, in_flat, extent, stride):
    whole_grad = lax.all_gather(grad_low, "chan", axis=3, tiled=True)
    result = spatial_scatter(matmul_back_t(whole_grad, in_flat), extent, stride)
    return result


def local(
    block_input,
    first_reduce,
    first_spatial,
    first_expand,
    first_shortcut,
    second_reduce,
    second_spatial,
    second_expand,
    first_mid_gain,
    first_mid_bias,
    first_wide_gain,
    first_wide_bias,
    second_mid_gain,
    second_mid_bias,
    second_wide_gain,
    second_wide_bias,
    subnet_widths,
    subnet_ids,
    crop_sides,
    cotangent,
):
    crop_count = block_input.shape[0]
    extent = block_input.shape[1]
    half_extent = extent // 2
    mid_local = first_reduce.shape[1]
    wide_local = first_shortcut.shape[1]
    chan_parts = lax.axis_size("chan")
    chan_place = lax.axis_index("chan")
    crop_start = lax.axis_index("batch") * crop_count
    local_sides = lax.dynamic_slice_in_dim(crop_sides, crop_start, crop_count)
    local_ids = lax.dynamic_slice_in_dim(subnet_ids, crop_start, crop_count)
    labels = jnp.arange(subnet_widths.shape[0], dtype=jnp.int32)
    member_all = (subnet_ids[None, :] == labels[:, None]).astype(jnp.float32)
    member = (local_ids[None, :] == labels[:, None]).astype(jnp.float32)
    halves_all = crop_sides // 2
    count_full = jnp.sum(
        member_all * (crop_sides * crop_sides).astype(jnp.float32)[None, :], axis=1
    )
    count_half = jnp.sum(
        member_all * (halves_all * halves_all).astype(jnp.float32)[None, :], axis=1
    )
    rows_full = jnp.arange(extent, dtype=jnp.int32)
    inside_full = (rows_full[None, :] < local_sides[:, None]).astype(jnp.float32)
    mask_full = inside_full[:, :, None] * inside_full[:, None, :]
    rows_half = jnp.arange(half_extent, dtype=jnp.int32)
    inside_half = (rows_half[None, :] < (local_sides // 2)[:, None]).astype(jnp.float32)
    mask_half = inside_half[:, :, None] * inside_half[:, None, :]
    crop_width = jnp.sum(member * subnet_widths.astype(jnp.float32)[:, None], axis=0)
    channel_index = (chan_place * mid_local + jnp.arange(mid_local, dtype=jnp.int32)).astype(
        jnp.float32
    )
    active = (channel_index[None, :] < crop_width[:, None]).astype(jnp.float32)
    keep_full = mask_full[..., None] * active[:, None, None, :]
    keep_half = mask_half[..., None] * active[:, None, None, :]
    reduce_one, spatial_one, expand_one, shortcut_one, reduce_two, spatial_two, expand_two = (
        lax.all_gather(first_reduce.astype(jnp.bfloat16), "batch", axis=0, tiled=True),
        lax.all_gather(first_spatial.astype(jnp.bfloat16), "batch", axis=2, tiled=True),
        lax.all_gather(first_expand.astype(jnp.bfloat16), "batch", axis=1, tiled=True),
        lax.all_gather(first_shortcut.astype(jnp.bfloat16), "batch", axis=0, tiled=True),
        lax.all_gather(second_reduce.astype(jnp.bfloat16), "batch", axis=0, tiled=True),
        lax.all_gather(second_spatial.astype(jnp.bfloat16), "batch", axis=2, tiled=True),
        lax.all_gather(second_expand.astype(jnp.bfloat16), "batch", axis=1, tiled=True),
    )
    spatial_one_flat = spatial_one.reshape(-1, mid_local)
    spatial_two_flat = spatial_two.reshape(-1, mid_local)

    def spatial_by_owner(weight):
        grouped = weight.reshape(3, 3, chan_parts, mid_local, mid_local).transpose(2, 4, 0, 1, 3)
        return grouped.reshape(chan_parts, mid_local, 9 * mid_local)

    def expand_by_owner(weight):
        return weight.reshape(mid_local, chan_parts, wide_local).transpose(1, 0, 2)

    expand_one_ex, expand_two_ex, spatial_one_ex, spatial_two_ex, reduce_two_ex = (
        lax.all_to_all(
            expand_by_owner(expand_one), "chan", split_axis=0, concat_axis=1, tiled=True
        ),
        lax.all_to_all(
            expand_by_owner(expand_two), "chan", split_axis=0, concat_axis=1, tiled=True
        ),
        lax.all_to_all(
            spatial_by_owner(spatial_one), "chan", split_axis=0, concat_axis=1, tiled=True
        ),
        lax.all_to_all(
            spatial_by_owner(spatial_two), "chan", split_axis=0, concat_axis=1, tiled=True
        ),
        lax.all_to_all(
            rows_by_owner(reduce_two, chan_parts), "chan", split_axis=0, concat_axis=1, tiled=True
        ),
    )
    expand_one_cols = expand_one_ex[0]
    expand_two_cols = expand_two_ex[0]
    spatial_one_back = spatial_one_ex[0]
    spatial_two_back = spatial_two_ex[0]
    reduce_two_rows = reduce_two_ex[0]
    masked_input = (block_input.astype(jnp.float32) * mask_full[..., None]).astype(jnp.bfloat16)
    whole_input = gather_features(masked_input)
    pre_one = matmul_last(whole_input, reduce_one)
    norm_one, cent_one, scale_one = norm_forward(
        pre_one, mask_full, member, count_full, first_mid_gain[0], first_mid_bias[0]
    )
    act_one = (jax.nn.silu(norm_one) * keep_full).astype(jnp.bfloat16)
    cols_one = spatial_columns(gather_mids(act_one), 2)
    pre_two = matmul_last(cols_one, spatial_one_flat)
    norm_two, cent_two, scale_two = norm_forward(
        pre_two, mask_half, member, count_half, first_mid_gain[1], first_mid_bias[1]
    )
    act_two = (jax.nn.silu(norm_two) * keep_half).astype(jnp.bfloat16)
    pre_three = expand_channels(act_two, expand_one_cols)
    short_in = whole_input[:, ::2, ::2, :]
    pre_short = matmul_last(short_in, shortcut_one)
    joined = jnp.concatenate([pre_three, pre_short], axis=3)
    norm_wide, cent_wide, scale_wide = norm_forward(
        joined,
        mask_half,
        member,
        count_half,
        first_wide_gain.reshape(-1),
        first_wide_bias.reshape(-1),
    )
    sum_one = norm_wide[..., :wide_local] + norm_wide[..., wide_local:]
    section_out = jax.nn.silu(sum_one) * mask_half[..., None]
    whole_section = gather_features(section_out.astype(jnp.bfloat16))
    pre_four = matmul_last(whole_section, reduce_two)
    norm_four, cent_four, scale_four = norm_forward(
        pre_four, mask_half, member, count_half, second_mid_gain[0], second_mid_bias[0]
    )
    act_four = (jax.nn.silu(norm_four) * keep_half).astype(jnp.bfloat16)
    cols_four = spatial_columns(gather_mids(act_four), 1)
    pre_five = matmul_last(cols_four, spatial_two_flat)
    norm_five, cent_five, scale_five = norm_forward(
        pre_five, mask_half, member, count_half, second_mid_gain[1], second_mid_bias[1]
    )
    act_five = (jax.nn.silu(norm_five) * keep_half).astype(jnp.bfloat16)
    pre_six = expand_channels(act_five, expand_two_cols)
    norm_six, cent_six, scale_six = norm_forward(
        pre_six, mask_half, member, count_half, second_wide_gain, second_wide_bias
    )
    sum_two = norm_six + section_out
    output = jax.nn.silu(sum_two) * mask_half[..., None]
    grad_final = cotangent.astype(jnp.float32) * mask_half[..., None] * silu_slope(sum_two)
    grad_six, wide_two_gain, wide_two_bias = norm_backward(
        grad_final, cent_six, scale_six, mask_half, member, count_half, second_wide_gain
    )
    whole_grad_six = gather_wide(grad_six.astype(jnp.bfloat16))
    expand_two_grad = weight_term(act_five, whole_grad_six)
    back_five = matmul_back(whole_grad_six, expand_two)
    grad_five, mid_five_gain, mid_five_bias = norm_backward(
        back_five * keep_half * silu_slope(norm_five),
        cent_five,
        scale_five,
        mask_half,
        member,
        count_half,
        second_mid_gain[1],
    )
    grad_five_low = grad_five.astype(jnp.bfloat16)
    spatial_two_grad = weight_term(cols_four, grad_five_low).reshape(spatial_two.shape)
    back_four = spatial_back(grad_five_low, spatial_two_back, half_extent, 1)
    grad_four, mid_four_gain, mid_four_bias = norm_backward(
        back_four * keep_half * silu_slope(norm_four),
        cent_four,
        scale_four,
        mask_half,
        member,
        count_half,
        second_mid_gain[0],
    )
    grad_four_low = grad_four.astype(jnp.bfloat16)
    reduce_two_grad = weight_term(whole_section, grad_four_low)
    whole_grad_four = lax.all_gather(grad_four_low, "chan", axis=3, tiled=True)
    back_section = matmul_back_t(whole_grad_four, reduce_two_rows) + grad_final
    grad_sum_one = back_section * mask_half[..., None] * silu_slope(sum_one)
    grad_joined, wide_one_gain, wide_one_bias = norm_backward(
        jnp.concatenate([grad_sum_one, grad_sum_one], axis=3),
        cent_wide,
        scale_wide,
        mask_half,
        member,
        count_half,
        first_wide_gain.reshape(-1),
    )
    grad_three_low = grad_joined[..., :wide_local].astype(jnp.bfloat16)
    grad_short_low = grad_joined[..., wide_local:].astype(jnp.bfloat16)
    whole_grad_three = gather_wide(grad_three_low)
    expand_one_grad = weight_term(act_two, whole_grad_three)
    shortcut_one_grad = weight_term(short_in, grad_short_low)
    back_two = matmul_back(whole_grad_three, expand_one)
    grad_two, mid_two_gain, mid_two_bias = norm_backward(
        back_two * keep_half * silu_slope(norm_two),
        cent_two,
        scale_two,
        mask_half,
        member,
        count_half,
        first_mid_gain[1],
    )
    grad_two_low = grad_two.astype(jnp.bfloat16)
    spatial_one_grad = weight_term(cols_one, grad_two_low).reshape(spatial_one.shape)
    back_one = spatial_back(grad_two_low, spatial_one_back, extent, 2)
    grad_one, mid_one_gain, mid_one_bias = norm_backward(
        back_one * keep_full * silu_slope(norm_one),
        cent_one,
        scale_one,
        mask_full,
        member,
        count_full,
        first_mid_gain[0],
    )
    grad_one_low = grad_one.astype(jnp.bfloat16)
    reduce_one_grad = weight_term(whole_input, grad_one_low)
    spread_pad = ((0, 0, 0), (0, 1, 1), (0, 1, 1), (0, 0, 0))
    from_reduce = matmul_back(grad_one_low, reduce_one)
    from_short = lax.pad(matmul_back(grad_short_low, shortcut_one), jnp.float32(0.0), spread_pad)
    input_grad = lax.psum_scatter(
        (from_reduce + from_short).astype(jnp.bfloat16), "chan", scatter_dimension=3, tiled=True
    ).astype(jnp.float32)
    input_grad = input_grad * mask_full[..., None]
    (
        reduce_one_out,
        spatial_one_out,
        expand_one_out,
        shortcut_one_out,
        reduce_two_out,
        spatial_two_out,
        expand_two_out,
    ) = (
        lax.psum_scatter(reduce_one_grad, "batch", scatter_dimension=0, tiled=True),
        lax.psum_scatter(spatial_one_grad, "batch", scatter_dimension=2, tiled=True),
        lax.psum_scatter(expand_one_grad, "batch", scatter_dimension=1, tiled=True),
        lax.psum_scatter(shortcut_one_grad, "batch", scatter_dimension=0, tiled=True),
        lax.psum_scatter(reduce_two_grad, "batch", scatter_dimension=0, tiled=True),
        lax.psum_scatter(spatial_two_grad, "batch", scatter_dimension=2, tiled=True),
        lax.psum_scatter(expand_two_grad, "batch", scatter_dimension=1, tiled=True),
    )
    return (
        output,
        input_grad,
        reduce_one_out,
        spatial_one_out,
        expand_one_out,
        shortcut_one_out,
        reduce_two_out,
        spatial_two_out,
        expand_two_out,
        jnp.stack([mid_one_gain, mid_two_gain]),
        jnp.stack([mid_one_bias, mid_two_bias]),
        wide_one_gain.reshape(2, wide_local),
        wide_one_bias.reshape(2, wide_local),
        jnp.stack([mid_four_gain, mid_five_gain]),
        jnp.stack([mid_four_bias, mid_five_bias]),
        wide_two_gain,
        wide_two_bias,
    )


def solution(mesh):
    placed = (
        P("batch", None, None, "chan"),
        P("batch", "chan"),
        P(None, None, "batch", "chan"),
        P("chan", "batch"),
        P("batch", "chan"),
        P("batch", "chan"),
        P(None, None, "batch", "chan"),
        P("chan", "batch"),
        P(None, "chan"),
        P(None, "chan"),
        P(None, "chan"),
        P(None, "chan"),
        P(None, "chan"),
        P(None, "chan"),
        P("chan"),
        P("chan"),
        P(),
        P(),
        P(),
        P("batch", None, None, "chan"),
    )
    return jax.shard_map(
        local,
        mesh=mesh,
        in_specs=placed,
        out_specs=(
            P("batch", None, None, "chan"),
            P("batch", None, None, "chan"),
            P("batch", "chan"),
            P(None, None, "batch", "chan"),
            P("chan", "batch"),
            P("batch", "chan"),
            P("batch", "chan"),
            P(None, None, "batch", "chan"),
            P("chan", "batch"),
            P(None, "chan"),
            P(None, "chan"),
            P(None, "chan"),
            P(None, "chan"),
            P(None, "chan"),
            P(None, "chan"),
            P("chan"),
            P("chan"),
        ),
        check_vma=False,
    )
```

profile of v0, /device:TPU:4, one launch (start us, length us, event | category | flops | bytes accessed | tf_op | source)
XLA Modules:
  0.0 1460.4 jit_solution(14520397649602888585)
XLA Ops:
  12.9 31.1 %all_gather.55 = bf16[1024,128]{1,0:T(8,128)(2,1)S(1)} all-gather(bf16[128,128]{1,0:T(8,128)(2,1)S(1)} %convert_element_type.122), channel_id=1, replica_groups=mesh['batch'=8,'chan'=4] {'batch'}, dimensions={0}, use_global_device_ids=true | all-gather | bytes 294912 | tf_op jit(solution)/shard_map/all_gather | solution.py:180
  44.4 14.9 %all-gather.9.cloned.1.call-done = bf16[16,14,14,1024]{3,0,2,1:T(8,128)(2,1)} async-done(((bf16[16,14,14,256]{3,0,2,1:T(8,128)(2,1)}), bf16[16,14,14,1024]{3,0,2,1:T(8,128)(2,1)}) %all-gather.9.cloned.1.call-update) | async-done | bytes 6422544 | tf_op jit(solution)/shard_map/all_gather | solution.py:101
  59.3 4.6 multiply_reduce_fusion.2
  64.2 21.6 %all-reduce.32 = (f32[3,128]{1,0:T(4,128)S(1)}, f32[3,128]{1,0:T(4,128)S(1)}) all-reduce(f32[3,128]{1,0:T(4,128)S(1)} %fusion.136, f32[3,128]{1,0:T(4,128)S(1)} %fusion.138), channel_id=1, replica_groups=mesh['batch'=8,'chan'=4] {'batch'}, use_global_device_ids=true, to_apply=%region_4.5 | all-reduce | flops 768 | bytes 6144 | tf_op jit(solution)/shard_map/psum | solution.py:77
  89.2 32.1 %all_gather.59 = bf16[128,2048]{1,0:T(8,128)(2,1)S(1)} all-gather(bf16[128,256]{1,0:T(8,128)(2,1)S(1)} %convert_element_type.132), channel_id=1, replica_groups=mesh['batch'=8,'chan'=4] {'batch'}, dimensions={1}, use_global_device_ids=true | all-gather | bytes 589824 | tf_op jit(solution)/shard_map/all_gather | solution.py:182
  122.9 4.5 all-to-all-start
  130.3 8.8 all-gather.11.cloned.1.call-done
  149.6 35.9 %all-gather.13.cloned.1.call-done = bf16[3,3,512,128]{3,2,1,0:T(8,128)(2,1)} async-done(((bf16[3,3,64,128]{3,2,1,0:T(8,128)(2,1)}), bf16[3,3,512,128]{3,2,1,0:T(8,128)(2,1)}) %all-gather.13.cloned.1.call-update) | async-done | bytes 1179664 | tf_op jit(solution)/shard_map/all_gather | solution.py:181
  185.5 5.3 multiply_reduce_fusion.7
  191.1 19.2 %all-reduce.31 = (f32[3,128]{1,0:T(4,128)S(1)}, f32[3,128]{1,0:T(4,128)S(1)}) all-reduce(f32[3,128]{1,0:T(4,128)S(1)} %fusion.133, f32[3,128]{1,0:T(4,128)S(1)} %fusion.135), channel_id=1, replica_groups=mesh['batch'=8,'chan'=4] {'batch'}, use_global_device_ids=true, to_apply=%region_10.11 | all-reduce | flops 768 | bytes 6144 | tf_op jit(solution)/shard_map/psum | solution.py:77
  211.5 8.2 all_gather.58
  223.2 33.1 %all-reduce.30 = (f32[3,1024]{1,0:T(4,128)S(1)}, f32[3,1024]{1,0:T(4,128)S(1)}) all-reduce(f32[3,1024]{1,0:T(4,128)S(1)} %fusion.130, f32[3,1024]{1,0:T(4,128)S(1)} %fusion.132), channel_id=1, replica_groups=mesh['batch'=8,'chan'=4] {'batch'}, use_global_device_ids=true, to_apply=%region_14.15 | all-reduce | flops 6144 | bytes 49152 | tf_op jit(solution)/shard_map/psum | solution.py:77
  262.5 31.2 %all_gather.66 = bf16[128,2048]{1,0:T(8,128)(2,1)S(1)} all-gather(bf16[128,256]{1,0:T(8,128)(2,1)S(1)} %convert_element_type.139), channel_id=1, replica_groups=mesh['batch'=8,'chan'=4] {'batch'}, dimensions={1}, use_global_device_ids=true | all-gather | bytes 589824 | tf_op jit(solution)/shard_map/all_gather | solution.py:186
  295.5 5.5 all-to-all-start.1
  303.6 34.2 %all_gather.62 = bf16[2048,128]{1,0:T(8,128)(2,1)} all-gather(bf16[256,128]{1,0:T(8,128)(2,1)S(1)} %convert_element_type.135), channel_id=1, replica_groups=mesh['batch'=8,'chan'=4] {'batch'}, dimensions={0}, use_global_device_ids=true | all-gather | bytes 589824 | tf_op jit(solution)/shard_map/all_gather | solution.py:184
  337.9 3.8 multiply_reduce_fusion.6
  342.0 17.1 %all-reduce.29 = (f32[3,128]{1,0:T(4,128)S(1)}, f32[3,128]{1,0:T(4,128)S(1)}) all-reduce(f32[3,128]{1,0:T(4,128)S(1)} %fusion.127, f32[3,128]{1,0:T(4,128)S(1)} %fusion.129), channel_id=1, replica_groups=mesh['batch'=8,'chan'=4] {'batch'}, use_global_device_ids=true, to_apply=%region_18.19 | all-reduce | flops 768 | bytes 6144 | tf_op jit(solution)/shard_map/psum | solution.py:77
  361.3 7.7 all_gather.63
  378.2 6.2 multiply_reduce_fusion.5
  384.6 19.1 %all-reduce.28 = (f32[3,128]{1,0:T(4,128)S(1)}, f32[3,128]{1,0:T(4,128)S(1)}) all-reduce(f32[3,128]{1,0:T(4,128)S(1)} %fusion.124, f32[3,128]{1,0:T(4,128)S(1)} %fusion.126), channel_id=1, replica_groups=mesh['batch'=8,'chan'=4] {'batch'}, use_global_device_ids=true, to_apply=%region_22.23 | all-reduce | flops 768 | bytes 6144 | tf_op jit(solution)/shard_map/psum | solution.py:77
  406.6 9.4 all_gather.65
  419.3 33.6 %all-reduce.27 = (f32[3,512]{1,0:T(4,128)}, f32[3,512]{1,0:T(4,128)}) all-reduce(f32[3,512]{1,0:T(4,128)S(1)} %fusion.121, f32[3,512]{1,0:T(4,128)S(1)} %fusion.123), channel_id=1, replica_groups=mesh['batch'=8,'chan'=4] {'batch'}, use_global_device_ids=true, to_apply=%region_26.27 | all-reduce | flops 3072 | bytes 24576 | tf_op jit(solution)/shard_map/psum | solution.py:77
  455.4 5.0 fusion.210
  461.8 33.8 %all-reduce.26 = (f32[3,512]{1,0:T(4,128)}, f32[3,512]{1,0:T(4,128)}) all-reduce(f32[3,512]{1,0:T(4,128)} %fusion.119, f32[3,512]{1,0:T(4,128)} %fusion.120), channel_id=1, replica_groups=mesh['batch'=8,'chan'=4] {'batch'}, use_global_device_ids=true, to_apply=%region_30.31 | all-reduce | flops 3072 | bytes 24576 | tf_op jit(solution)/shard_map/psum | solution.py:90
  500.8 4.5 all-to-all-start.3
  507.8 10.2 all-to-all-done.3
  518.0 6.0 all-to-all-start.2
  526.2 16.2 %all-to-all-done.2 = bf16[4,128,1152]{1,2,0:T(8,128)(2,1)} async-done(((bf16[4,128,1152]{1,2,0:T(8,128)(2,1)}), bf16[4,128,1152]{1,2,0:T(8,128)(2,1)}, u32[]{:S(2)}, u32[]{:S(2)}) %all-to-all-start.2) | async-done | bytes 1179680 | tf_op jit(solution)/shard_map/all_to_all | solution.py:208
  544.8 4.0 fusion.213
  549.0 17.7 %all-reduce.25 = (f32[3,128]{1,0:T(4,128)}, f32[3,128]{1,0:T(4,128)S(1)}) all-reduce(f32[3,128]{1,0:T(4,128)S(1)} %fusion.117, f32[3,128]{1,0:T(4,128)S(1)} %fusion.118), channel_id=1, replica_groups=mesh['batch'=8,'chan'=4] {'batch'}, use_global_device_ids=true, to_apply=%region_34.35 | all-reduce | flops 768 | bytes 6144 | tf_op jit(solution)/shard_map/psum | solution.py:90
  569.9 8.9 all_gather.68
  582.7 19.2 %all-reduce.24 = (f32[3,128]{1,0:T(4,128)S(1)}, f32[3,128]{1,0:T(4,128)S(1)}) all-reduce(f32[3,128]{1,0:T(4,128)S(1)} %fusion.115, f32[3,128]{1,0:T(4,128)S(1)} %fusion.116), channel_id=1, replica_groups=mesh['batch'=8,'chan'=4] {'batch'}, use_global_device_ids=true, to_apply=%region_38.39 | all-reduce | flops 768 | bytes 6144 | tf_op jit(solution)/shard_map/psum | solution.py:90
  603.8 7.6 all_gather.69
  615.7 33.9 %all-reduce.23 = (f32[3,1024]{1,0:T(4,128)}, f32[3,1024]{1,0:T(4,128)S(1)}) all-reduce(f32[3,1024]{1,0:T(4,128)S(1)} %fusion.113, f32[3,1024]{1,0:T(4,128)S(1)} %fusion.114), channel_id=1, replica_groups=mesh['batch'=8,'chan'=4] {'batch'}, use_global_device_ids=true, to_apply=%region_42.43 | all-reduce | flops 6144 | bytes 49152 | tf_op jit(solution)/shard_map/psum | solution.py:90
  656.0 30.9 %all_to_all.20 = bf16[4,128,1152]{1,2,0:T(8,128)(2,1)S(1)} all-to-all(bf16[4,128,1152]{1,2,0:T(8,128)(2,1)S(1)} %bitcast.211), channel_id=1, replica_groups=mesh['batch'=8,'chan'=4] {'chan'}, dimensions={0} | all-to-all | bytes 2359296 | tf_op jit(solution)/shard_map/all_to_all | solution.py:205
  690.8 20.1 %pad.85 = f32[16,14,14,1024]{3,0,2,1:T(8,128)} pad(f32[16,7,7,1024]{3,0,2,1:T(8,128)S(1)} %fusion.21, f32[]{:T(128)} %constant.54.clone.1), padding=0_0_0x0_1_1x0_1_1x0_0_0 | pad | bytes 16056324 | tf_op jit(solution)/shard_map/pad | solution.py:338
  714.5 17.3 %all-reduce.22 = (f32[3,128]{1,0:T(4,128)S(1)}, f32[3,128]{1,0:T(4,128)S(1)}) all-reduce(f32[3,128]{1,0:T(4,128)S(1)} %fusion.111, f32[3,128]{1,0:T(4,128)S(1)} %fusion.112), channel_id=1, replica_groups=mesh['batch'=8,'chan'=4] {'batch'}, use_global_device_ids=true, to_apply=%region_46.47 | all-reduce | flops 768 | bytes 6144 | tf_op jit(solution)/shard_map/psum | solution.py:90
  732.4 8.9 all_gather.71
  743.7 16.0 %pad.109 = f32[16,14,14,128]{3,0,2,1:T(8,128)} pad(f32[16,7,7,128]{3,0,2,1:T(8,128)S(1)} %get-tuple-element.75, f32[]{:T(128)} %constant.54.clone.1), padding=0_0_0x1_0_1x1_0_1x0_0_0 | pad | bytes 2007044 | tf_op jit(solution)/shard_map/slice | solution.py:70
  759.6 16.0 %pad.108 = f32[16,14,14,128]{3,0,2,1:T(8,128)} pad(f32[16,7,7,128]{3,0,2,1:T(8,128)S(1)} %get-tuple-element.76, f32[]{:T(128)} %constant.54.clone.1), padding=0_0_0x1_0_1x0_1_1x0_0_0 | pad | bytes 2007044 | tf_op jit(solution)/shard_map/slice | solution.py:70
  775.6 16.1 %pad.106 = f32[16,14,14,128]{3,0,2,1:T(8,128)} pad(f32[16,7,7,128]{3,0,2,1:T(8,128)S(1)} %get-tuple-element.78, f32[]{:T(128)} %constant.54.clone.1), padding=0_0_0x0_1_1x1_0_1x0_0_0 | pad | bytes 2007044 | tf_op jit(solution)/shard_map/slice | solution.py:70
  791.7 16.0 %pad.105 = f32[16,14,14,128]{3,0,2,1:T(8,128)} pad(f32[16,7,7,128]{3,0,2,1:T(8,128)S(1)} %get-tuple-element.79, f32[]{:T(128)} %constant.54.clone.1), padding=0_0_0x0_1_1x0_1_1x0_0_0 | pad | bytes 2007044 | tf_op jit(solution)/shard_map/slice | solution.py:70
  807.7 16.1 %pad.77 = f32[16,16,16,128]{3,0,2,1:T(8,128)} pad(f32[16,7,7,128]{3,0,2,1:T(8,128)S(1)} %get-tuple-element.74, f32[]{:T(128)} %constant.54.clone.1), padding=0_0_0x0_3_1x1_2_1x0_0_0 | pad | bytes 2498564 | tf_op jit(solution)/shard_map/pad | solution.py:60
  824.4 16.0 %pad.239 = f32[16,14,15,128]{3,0,2,1:T(8,128)} pad(f32[16,7,7,128]{3,0,2,1:T(8,128)S(1)} %get-tuple-element.80, f32[]{:T(128)} %constant.54.clone.1), padding=0_0_0x0_1_1x0_2_1x0_0_0 | pad | bytes 2121732
  840.4 16.2 %pad.78 = f32[16,16,16,128]{3,0,2,1:T(8,128)} pad(f32[16,7,7,128]{3,0,2,1:T(8,128)S(1)} %copy-done.24, f32[]{:T(128)} %constant.54.clone.1), padding=0_0_0x0_3_1x2_1_1x0_0_0 | pad | bytes 2498564 | tf_op jit(solution)/shard_map/pad | solution.py:60
  856.6 16.3 %pad.76 = f32[16,16,16,128]{3,0,2,1:T(8,128)} pad(f32[16,7,7,128]{3,0,2,1:T(8,128)S(1)} %copy-done.23, f32[]{:T(128)} %constant.54.clone.1), padding=0_0_0x0_3_1x0_3_1x0_0_0 | pad | bytes 2498564 | tf_op jit(solution)/shard_map/pad | solution.py:60
  872.9 3.5 add_add_fusion
  878.2 3.7 fusion.209
  882.1 19.1 %all-reduce.21 = (f32[3,128]{1,0:T(4,128)S(1)}, f32[3,128]{1,0:T(4,128)S(1)}) all-reduce(f32[3,128]{1,0:T(4,128)S(1)} %fusion.109, f32[3,128]{1,0:T(4,128)S(1)} %fusion.110), channel_id=1, replica_groups=mesh['batch'=8,'chan'=4] {'batch'}, use_global_device_ids=true, to_apply=%region_50.51 | all-reduce | flops 768 | bytes 6144 | tf_op jit(solution)/shard_map/psum | solution.py:90
  903.6 9.4 add_convert_fusion
  917.7 5.0 convolution_bitcast_fusion.1
  923.1 4.2 convolution_bitcast_fusion.3
  928.2 6.9 fusion.223
  935.1 5.8 convolution_bitcast_fusion.4
  943.8 6.9 fusion.222
  956.3 12.3 reduce-scatter.9.cloned.1.call-done
  968.6 3.6 convert_multiply_fusion
  972.1 65.7 %reduce-scatter.23.cloned.1.call-done = f32[128,256]{1,0:T(8,128)} async-done(((f32[128,2048]{1,0:T(8,128)}), f32[128,256]{1,0:T(8,128)}) %reduce-scatter.23.cloned.1.call-update) | async-done | bytes 131088 | tf_op jit(solution)/shard_map/reduce_scatter | solution.py:358
  1037.8 66.5 %reduce-scatter.19.cloned.1.call-done = f32[256,128]{1,0:T(8,128)} async-done(((f32[2048,128]{1,0:T(8,128)}), f32[256,128]{1,0:T(8,128)}) %reduce-scatter.19.cloned.1.call-update) | async-done | bytes 131088 | tf_op jit(solution)/shard_map/reduce_scatter | solution.py:356
  1104.3 71.2 %reduce-scatter.17.cloned.1.call-done = f32[128,512]{1,0:T(8,128)} async-done(((f32[1024,512]{1,0:T(8,128)}), f32[128,512]{1,0:T(8,128)}) %reduce-scatter.17.cloned.1.call-update) | async-done | bytes 262160 | tf_op jit(solution)/shard_map/reduce_scatter | solution.py:355
  1175.5 73.2 %reduce-scatter.21.cloned.1.call-done = f32[3,3,64,128]{3,2,1,0:T(8,128)} async-done(((f32[3,3,512,128]{3,2,1,0:T(8,128)}), f32[3,3,64,128]{3,2,1,0:T(8,128)}) %reduce-scatter.21.cloned.1.call-update) | async-done | bytes 294928 | tf_op jit(solution)/shard_map/reduce_scatter | solution.py:357
  1248.7 65.1 %reduce-scatter.11.cloned.1.call-done = f32[128,128]{1,0:T(8,128)} async-done(((f32[1024,128]{1,0:T(8,128)}), f32[128,128]{1,0:T(8,128)}) %reduce-scatter.11.cloned.1.call-update) | async-done | bytes 65552 | tf_op jit(solution)/shard_map/reduce_scatter | solution.py:352
  1313.9 66.7 %reduce-scatter.15.cloned.1.call-done = f32[128,256]{1,0:T(8,128)} async-done(((f32[128,2048]{1,0:T(8,128)}), f32[128,256]{1,0:T(8,128)}) %reduce-scatter.15.cloned.1.call-update) | async-done | bytes 131088 | tf_op jit(solution)/shard_map/reduce_scatter | solution.py:354
  1380.6 72.9 %reduce-scatter.13.cloned.1.call-done = f32[3,3,64,128]{3,2,1,0:T(8,128)} async-done(((f32[3,3,512,128]{3,2,1,0:T(8,128)}), f32[3,3,64,128]{3,2,1,0:T(8,128)}) %reduce-scatter.13.cloned.1.call-update) | async-done | bytes 294928 | tf_op jit(solution)/shard_map/reduce_scatter | solution.py:353
  (376 shorter events, 123.2 us)
Async XLA Ops:
  7.2 52.1 %all-gather.9.cloned.1.call-start = ((), (), s32[]{:S(2)}) async-start(), calls=%async_computation.13 | async-start | bytes 8028160 | tf_op jit(solution)/shard_map/all_gather | solution.py:101
  11.1 33.0 %copy-start.83 = (f32[2,128]{1,0:T(2,128)S(1)}, f32[2,128]{1,0:T(2,128)}, u32[]{:S(2)}) copy-start(f32[2,128]{1,0:T(2,128)} %param.29) | copy-start | bytes 3076
  11.1 33.0 %copy-start.84 = (f32[2,128]{1,0:T(2,128)S(1)}, f32[2,128]{1,0:T(2,128)}, u32[]{:S(2)}) copy-start(f32[2,128]{1,0:T(2,128)} %param.28) | copy-start | bytes 3076
  11.1 116.4 %all-gather.15.cloned.1.call-start = ((), (), s32[]{:S(2)}) async-start(), calls=%async_computation.16 | async-start | bytes 1179648 | tf_op jit(solution)/shard_map/all_gather | solution.py:183
  12.7 126.4 %all-gather.11.cloned.1.call-start = ((), (), s32[]{:S(2)}) async-start(), calls=%async_computation.14 | async-start | bytes 4014080 | tf_op jit(solution)/shard_map/all_gather | solution.py:105
  44.0 20.0 %copy-start.28 = (bf16[1024,128]{1,0:T(8,128)(2,1)}, bf16[1024,128]{1,0:T(8,128)(2,1)S(1)}, u32[]{:S(2)}) copy-start(bf16[1024,128]{1,0:T(8,128)(2,1)S(1)} %all_gather.55) | copy-start | bytes 786436
  44.1 42.8 %copy-start.59 = (f32[128]{0:T(128)}, f32[128]{0:T(128)S(1)}, u32[]{:S(2)}) copy-start(f32[128]{0:T(128)S(1)} %get-tuple-element.122) | copy-start | bytes 1540
  44.1 167.2 %copy-start.68 = (f32[128]{0:T(128)}, f32[128]{0:T(128)S(1)}, u32[]{:S(2)}) copy-start(f32[128]{0:T(128)S(1)} %get-tuple-element.99) | copy-start | bytes 1540
  44.1 167.2 %copy-start.70 = (f32[128]{0:T(128)}, f32[128]{0:T(128)S(1)}, u32[]{:S(2)}) copy-start(f32[128]{0:T(128)S(1)} %get-tuple-element.123) | copy-start | bytes 1540
  44.3 41.7 %copy-start.88 = (f32[3]{0:T(128)}, f32[3]{0:T(128)S(1)}, u32[]{:S(2)}) copy-start(f32[3]{0:T(128)S(1)} %get-tuple-element.42) | copy-start | bytes 40
  44.4 359.6 %copy-start.90 = (f32[3]{0:T(128)}, f32[3]{0:T(128)S(1)}, u32[]{:S(2)}) copy-start(f32[3]{0:T(128)S(1)} %get-tuple-element.41) | copy-start | bytes 40
  64.0 24.4 %copy-start.1 = (f32[16,14,14,128]{3,0,2,1:T(8,128)}, f32[16,14,14,128]{3,0,2,1:T(8,128)S(1)}, u32[]{:S(2)}) copy-start(f32[16,14,14,128]{3,0,2,1:T(8,128)S(1)} %get-tuple-element.103) | copy-start | bytes 4816900
  88.4 97.1 %all-gather.13.cloned.1.call-start = ((), (), s32[]{:S(2)}) async-start(), calls=%async_computation.15 | async-start | bytes 1327104 | tf_op jit(solution)/shard_map/all_gather | solution.py:181
  89.2 38.3 %copy-start.65 = (f32[2,512]{1,0:T(2,128)S(1)}, f32[2,512]{1,0:T(2,128)}, u32[]{:S(2)}) copy-start(f32[2,512]{1,0:T(2,128)} %param.30) | copy-start | bytes 12292
  89.2 38.3 %copy-start.66 = (f32[2,512]{1,0:T(2,128)S(1)}, f32[2,512]{1,0:T(2,128)}, u32[]{:S(2)}) copy-start(f32[2,512]{1,0:T(2,128)} %param.31) | copy-start | bytes 12292
  122.9 96.9 %all-to-all-start = ((bf16[4,128,512]{2,1,0:T(8,128)(2,1)}), bf16[4,128,512]{2,1,0:T(8,128)(2,1)S(1)}, u32[]{:S(2)}, u32[]{:S(2)}) async-start(bf16[4,128,512]{2,1,0:T(8,128)(2,1)} %bitcast.209), calls=%async_computation | async-start | bytes 1048576 | tf_op jit(solution)/shard_map/all_to_all | solution.py:199
  127.5 210.4 %all-gather.17.cloned.1.call-start = ((), (), s32[]{:S(2)}) async-start(), calls=%async_computation.17 | async-start | bytes 4014080 | tf_op jit(solution)/shard_map/all_gather | solution.py:101
  190.9 28.9 %copy-start.25 = (f32[16,7,7,128]{3,0,2,1:T(8,128)}, f32[16,7,7,128]{3,0,2,1:T(8,128)S(1)}, u32[]{:S(2)}) copy-start(f32[16,7,7,128]{3,0,2,1:T(8,128)S(1)} %get-tuple-element.104) | copy-start | bytes 1204228
  210.5 10.1 copy-start.44
  294.6 43.2 %copy-start.85 = (f32[2,128]{1,0:T(2,128)S(1)}, f32[2,128]{1,0:T(2,128)}, u32[]{:S(2)}) copy-start(f32[2,128]{1,0:T(2,128)} %param.33) | copy-start | bytes 3076
  294.6 43.2 %copy-start.86 = (f32[2,128]{1,0:T(2,128)S(1)}, f32[2,128]{1,0:T(2,128)}, u32[]{:S(2)}) copy-start(f32[2,128]{1,0:T(2,128)} %param.32) | copy-start | bytes 3076
  295.5 120.5 %all-to-all-start.1 = ((bf16[4,128,512]{2,1,0:T(8,128)(2,1)}), bf16[4,128,512]{2,1,0:T(8,128)(2,1)}, u32[]{:S(2)}, u32[]{:S(2)}) async-start(bf16[4,128,512]{2,1,0:T(8,128)(2,1)} %bitcast.219), calls=%async_computation.1 | async-start | bytes 1048576 | tf_op jit(solution)/shard_map/all_to_all | solution.py:202
  301.0 77.2 %all-gather.19.cloned.1.call-start = ((), (), s32[]{:S(2)}) async-start(), calls=%async_computation.18 | async-start | bytes 1327104 | tf_op jit(solution)/shard_map/all_gather | solution.py:185
  302.7 242.1 %all-gather.21.cloned.1.call-start = ((), (), s32[]{:S(2)}) async-start(), calls=%async_computation.19 | async-start | bytes 4014080 | tf_op jit(solution)/shard_map/all_gather | solution.py:109
  337.8 22.3 %copy-start.61 = (f32[128]{0:T(128)}, f32[128]{0:T(128)S(1)}, u32[]{:S(2)}) copy-start(f32[128]{0:T(128)S(1)} %get-tuple-element.96) | copy-start | bytes 1540
  337.8 22.3 %copy-start.63 = (f32[128]{0:T(128)}, f32[128]{0:T(128)S(1)}, u32[]{:S(2)}) copy-start(f32[128]{0:T(128)S(1)} %get-tuple-element.124) | copy-start | bytes 1540
  337.8 66.9 %copy-start.72 = (f32[128]{0:T(128)}, f32[128]{0:T(128)S(1)}, u32[]{:S(2)}) copy-start(f32[128]{0:T(128)S(1)} %get-tuple-element.95) | copy-start | bytes 1540
  337.9 66.9 %copy-start.74 = (f32[128]{0:T(128)}, f32[128]{0:T(128)S(1)}, u32[]{:S(2)}) copy-start(f32[128]{0:T(128)S(1)} %get-tuple-element.125) | copy-start | bytes 1540
  416.0 37.8 %copy-start.67 = (f32[512]{0:T(512)S(1)}, f32[512]{0:T(512)}, u32[]{:S(2)}) copy-start(f32[512]{0:T(512)} %param.34) | copy-start | bytes 6148
  500.8 17.2 %all-to-all-start.3 = ((bf16[4,128,512]{1,2,0:T(8,128)(2,1)}), bf16[4,128,512]{1,2,0:T(8,128)(2,1)}, u32[]{:S(2)}, u32[]{:S(2)}) async-start(bf16[4,128,512]{1,2,0:T(8,128)(2,1)} %bitcast.218), calls=%async_computation.3 | async-start | bytes 1048576 | tf_op jit(solution)/shard_map/all_to_all | solution.py:211
  518.0 24.4 %all-to-all-start.2 = ((bf16[4,128,1152]{1,2,0:T(8,128)(2,1)}), bf16[4,128,1152]{1,2,0:T(8,128)(2,1)}, u32[]{:S(2)}, u32[]{:S(2)}) async-start(bf16[4,128,1152]{1,2,0:T(8,128)(2,1)} %bitcast.210), calls=%async_computation.2 | async-start | bytes 2359296 | tf_op jit(solution)/shard_map/all_to_all | solution.py:208
  524.0 20.7 %copy-start.49 = (f32[16,128]{1,0:T(8,128)S(1)}, f32[16,128]{1,0:T(8,128)}, u32[]{:S(2)}) copy-start(f32[16,128]{1,0:T(8,128)} %copy-done.48) | copy-start | bytes 24580
  524.0 20.7 %copy-start.51 = (f32[16,128]{1,0:T(8,128)S(1)}, f32[16,128]{1,0:T(8,128)}, u32[]{:S(2)}) copy-start(f32[16,128]{1,0:T(8,128)} %copy-done.50) | copy-start | bytes 24580
  524.0 20.7 %copy-start.73 = (f32[128]{0:T(128)S(1)}, f32[128]{0:T(128)}, u32[]{:S(2)}) copy-start(f32[128]{0:T(128)} %copy-done.72) | copy-start | bytes 1540
  524.0 20.7 %copy-start.75 = (f32[128]{0:T(128)S(1)}, f32[128]{0:T(128)}, u32[]{:S(2)}) copy-start(f32[128]{0:T(128)} %copy-done.74) | copy-start | bytes 1540
  524.1 186.9 %all-gather.23.cloned.1.call-start = ((), (), s32[]{:S(2)}) async-start(), calls=%async_computation.20 | async-start | bytes 4014080 | tf_op jit(solution)/shard_map/all_gather | solution.py:109
  544.8 23.8 %copy-start.56 = (f32[16,128]{1,0:T(8,128)S(1)}, f32[16,128]{1,0:T(8,128)}, u32[]{:S(2)}) copy-start(f32[16,128]{1,0:T(8,128)} %get-tuple-element.111) | copy-start | bytes 24580
  566.7 13.3 copy-start.76
  566.7 12.1 copy-start.15
  581.3 20.5 %copy-start.91 = (f32[3]{0:T(128)S(1)}, f32[3]{0:T(128)}, u32[]{:S(2)}) copy-start(f32[3]{0:T(128)} %copy-done.90) | copy-start | bytes 40
  581.3 21.0 %copy-start.55 = (f32[16,128]{1,0:T(8,128)S(1)}, f32[16,128]{1,0:T(8,128)}, u32[]{:S(2)}) copy-start(f32[16,128]{1,0:T(8,128)} %get-tuple-element.113) | copy-start | bytes 24580
  601.8 12.5 copy-start.79
  601.8 12.5 copy-start.81
  601.8 9.6 copy-start.9
  614.3 35.3 %copy-start.92 = (f32[3]{0:T(128)S(1)}, f32[3]{0:T(128)}, u32[]{:S(2)}) copy-start(f32[3]{0:T(128)} %copy-done.90) | copy-start | bytes 40
  655.4 313.2 %reduce-scatter.9.cloned.1.call-start = ((), (), s32[]{:S(2)}) async-start(), calls=%async_computation.21 | async-start | bytes 8028160 | tf_op jit(solution)/shard_map/reduce_scatter | solution.py:339
  690.8 20.2 %copy-start.45 = (f32[16,128]{1,0:T(8,128)S(1)}, f32[16,128]{1,0:T(8,128)}, u32[]{:S(2)}) copy-start(f32[16,128]{1,0:T(8,128)} %copy-done.44) | copy-start | bytes 24580
  690.8 20.2 %copy-start.47 = (f32[16,128]{1,0:T(8,128)S(1)}, f32[16,128]{1,0:T(8,128)}, u32[]{:S(2)}) copy-start(f32[16,128]{1,0:T(8,128)} %copy-done.46) | copy-start | bytes 24580
  690.8 20.2 %copy-start.69 = (f32[128]{0:T(128)S(1)}, f32[128]{0:T(128)}, u32[]{:S(2)}) copy-start(f32[128]{0:T(128)} %copy-done.68) | copy-start | bytes 1540
  690.8 20.2 %copy-start.71 = (f32[128]{0:T(128)S(1)}, f32[128]{0:T(128)}, u32[]{:S(2)}) copy-start(f32[128]{0:T(128)} %copy-done.70) | copy-start | bytes 1540
  711.0 21.2 %copy-start.26 = (f32[16,7,7,128]{3,0,2,1:T(8,128)S(1)}, f32[16,7,7,128]{3,0,2,1:T(8,128)}, u32[]{:S(2)}) copy-start(f32[16,7,7,128]{3,0,2,1:T(8,128)} %copy-done.25) | copy-start | bytes 1204228
  711.0 21.2 %copy-start.54 = (f32[16,128]{1,0:T(8,128)S(1)}, f32[16,128]{1,0:T(8,128)}, u32[]{:S(2)}) copy-start(f32[16,128]{1,0:T(8,128)} %get-tuple-element.118) | copy-start | bytes 24580
  714.2 27.1 %copy-start.14 = (bf16[4,128,1152]{2,1,0:T(8,128)(2,1)S(1)}, bf16[4,128,1152]{2,1,0:T(8,128)(2,1)}, u32[]{:S(2)}) copy-start(bf16[4,128,1152]{2,1,0:T(8,128)(2,1)} %copy.60) | copy-start | bytes 3538948
  823.8 16.6 %copy-start.24 = (f32[16,7,7,128]{3,0,2,1:T(8,128)S(1)}, f32[16,7,7,128]{3,0,2,1:T(8,128)}, u32[]{:S(2)}) copy-start(f32[16,7,7,128]{3,0,2,1:T(8,128)} %get-tuple-element.81) | copy-start | bytes 1204228
  840.4 16.2 %copy-start.23 = (f32[16,7,7,128]{3,0,2,1:T(8,128)S(1)}, f32[16,7,7,128]{3,0,2,1:T(8,128)}, u32[]{:S(2)}) copy-start(f32[16,7,7,128]{3,0,2,1:T(8,128)} %get-tuple-element.82) | copy-start | bytes 1204228
  878.1 23.1 %copy-start.89 = (f32[3]{0:T(128)S(1)}, f32[3]{0:T(128)}, u32[]{:S(2)}) copy-start(f32[3]{0:T(128)} %copy-done.88) | copy-start | bytes 40
  878.1 23.5 %copy-start.53 = (f32[16,128]{1,0:T(8,128)S(1)}, f32[16,128]{1,0:T(8,128)}, u32[]{:S(2)}) copy-start(f32[16,128]{1,0:T(8,128)} %get-tuple-element.120) | copy-start | bytes 24580
  913.1 124.8 %reduce-scatter.23.cloned.1.call-start = ((), (), s32[]{:S(2)}) async-start(), calls=%async_computation.28 | async-start | bytes 1179648 | tf_op jit(solution)/shard_map/reduce_scatter | solution.py:358
  917.7 186.7 %reduce-scatter.19.cloned.1.call-start = ((), (), s32[]{:S(2)}) async-start(), calls=%async_computation.26 | async-start | bytes 1179648 | tf_op jit(solution)/shard_map/reduce_scatter | solution.py:356
  922.7 252.8 %reduce-scatter.17.cloned.1.call-start = ((), (), s32[]{:S(2)}) async-start(), calls=%async_computation.25 | async-start | bytes 2359296 | tf_op jit(solution)/shard_map/reduce_scatter | solution.py:355
  927.3 321.5 %reduce-scatter.21.cloned.1.call-start = ((), (), s32[]{:S(2)}) async-start(), calls=%async_computation.27 | async-start | bytes 2654208 | tf_op jit(solution)/shard_map/reduce_scatter | solution.py:357
  935.1 378.8 %reduce-scatter.11.cloned.1.call-start = ((), (), s32[]{:S(2)}) async-start(), calls=%async_computation.22 | async-start | bytes 589824 | tf_op jit(solution)/shard_map/reduce_scatter | solution.py:352
  941.0 439.6 %reduce-scatter.15.cloned.1.call-start = ((), (), s32[]{:S(2)}) async-start(), calls=%async_computation.24 | async-start | bytes 1179648 | tf_op jit(solution)/shard_map/reduce_scatter | solution.py:354
  943.8 509.7 %reduce-scatter.13.cloned.1.call-start = ((), (), s32[]{:S(2)}) async-start(), calls=%async_computation.23 | async-start | bytes 2654208 | tf_op jit(solution)/shard_map/reduce_scatter | solution.py:353
  (52 other events, 165.2 us)
Sparse Core Ops, SparseCore 0:
  11.3 48.0 all-gather.8
  62.0 44.6 all-gather.14
  108.9 30.1 all-gather.10
  141.7 43.7 all-gather.12
  261.7 24.9 all-gather.16
  304.3 40.1 all-gather.18
  500.9 34.2 all-gather.20
  655.5 37.5 all-gather.22
  913.2 55.2 reduce-scatter.8
  972.8 65.0 reduce-scatter.22
  1041.8 62.4 reduce-scatter.18
  1108.7 66.7 reduce-scatter.16
  1180.0 68.6 reduce-scatter.20
  1252.8 60.9 reduce-scatter.10
  1317.7 62.8 reduce-scatter.14
  1384.9 68.4 reduce-scatter.12
where the time goes:
time: 1470 us; the launch traced here: 1460 us
  waiting for transfers between devices  580 us (39%)
  blocking collectives  495 us (34%)
  local copies, waits for them, and re-layouts  196 us (13%)
  matrix products  105 us (7%)
  other arithmetic  48.3 us (3%)
  starting transfers between devices  21.4 us (1%)
  between operations  15.5 us (1%)
    psum x6, blocking collectives, norm_forward(): first_total, second_total = lax.psum((first_local, second_local), 'batch')  144 us
    psum x6, blocking collectives, norm_backward(): bias_total, gain_total = lax.psum((bias_local, gain_local), 'batch')  141 us
    reduce_scatter x1, waiting for transfers between devices, local(): lax.psum_scatter(spatial_two_grad, 'batch', scatter_dimension=2, tiled=True)  73.2 us
    reduce_scatter x1, waiting for transfers between devices, local(): lax.psum_scatter(spatial_one_grad, 'batch', scatter_dimension=2, tiled=True)  72.9 us
    reduce_scatter x1, waiting for transfers between devices, local(): lax.psum_scatter(shortcut_one_grad, 'batch', scatter_dimension=0, tiled=T...  71.2 us
    reduce_scatter x1, waiting for transfers between devices, local(): lax.psum_scatter(expand_one_grad, 'batch', scatter_dimension=1, tiled=True)  66.7 us
    reduce_scatter x1, waiting for transfers between devices, local(): lax.psum_scatter(reduce_two_grad, 'batch', scatter_dimension=0, tiled=True)  66.5 us
    reduce_scatter x1, waiting for transfers between devices, local(): lax.psum_scatter(expand_two_grad, 'batch', scatter_dimension=1, tiled=True)  65.7 us
  transfers between devices with their start and end apart: 20, of which 13 were waited for; matrix products, arithmetic and copies ran while one was open for 9% of the time, Pallas kernels for 0%

commit v1 on v0

v1 whole, which is shorter than its diff:
```python
import functools

import jax
import jax.numpy as jnp
import numpy as np
from jax import lax
from jax.experimental import pallas as pl
from jax.experimental.pallas import tpu as pltpu
from jax.sharding import PartitionSpec as P

F32, BF16 = jnp.float32, jnp.bfloat16
EPS = 1e-05
SMALL = 6
ALL = ("batch", "chan")


def silu_slope(v):
    s = jax.nn.sigmoid(v)
    return s * (1.0 + v * (1.0 - s))


class Geometry:
    def __init__(self, crops, side):
        self.crops, self.side = crops, side
        self.half, self.small = side // 2, SMALL // 2
        self.images = crops // 8
        self.large_n, self.small_n = 2 * self.images, 6 * self.images
        order = [8 * m + k for m in range(self.images) for k in range(2)]
        order += [8 * m + k for m in range(self.images) for k in range(2, 8)]
        rows = []
        for n, crop in enumerate(order):
            extent = self.half if n < self.large_n else self.small
            rows += [(crop, i, j) for i in range(extent) for j in range(extent)]
        self.rows = np.array(rows, np.int32)
        self.pixels = len(rows)
        where = {tuple(r): n for n, r in enumerate(rows)}
        shifts = np.zeros((9, self.pixels, self.pixels), np.float32)
        for n, (crop, i, j) in enumerate(rows):
            for tap in range(9):
                src = where.get((crop, i + tap // 3 - 1, j + tap % 3 - 1))
                if src is not None:
                    shifts[tap, n, src] = 1.0
        self.shifts = shifts

    def split(self, x):
        x = x.reshape((self.images, 8) + x.shape[1:])
        large = x[:, :2].reshape((self.large_n,) + x.shape[2:])
        small = x[:, 2:].reshape((self.small_n,) + x.shape[2:])
        return large, small

    def pack_full(self, x):
        c = x.shape[-1]
        large, small = self.split(x)
        small = small[:, :SMALL, :SMALL]
        h, s = self.half, self.small
        large = large.reshape(self.large_n, h, 2, h, 2, c).transpose(2, 4, 0, 1, 3, 5)
        small = small.reshape(self.small_n, s, 2, s, 2, c).transpose(2, 4, 0, 1, 3, 5)
        return jnp.concatenate([large.reshape(4, -1, c), small.reshape(4, -1, c)], axis=1)

    def pack_half(self, x):
        c = x.shape[-1]
        large, small = self.split(x)
        small = small[:, : self.small, : self.small]
        return jnp.concatenate([large.reshape(-1, c), small.reshape(-1, c)], axis=0)

    def join(self, large, small):
        tail = large.shape[1:]
        large = large.reshape((self.images, 2) + tail)
        small = small.reshape((self.images, 6) + tail)
        return jnp.concatenate([large, small], axis=1).reshape((self.crops,) + tail)

    def unpack_half(self, x):
        c = x.shape[-1]
        h, s = self.half, self.small
        cut = self.large_n * h * h
        large = x[:cut].reshape(self.large_n, h, h, c)
        small = x[cut:].reshape(self.small_n, s, s, c)
        small = jnp.pad(small, ((0, 0), (0, h - s), (0, h - s), (0, 0)))
        return self.join(large, small)

    def unpack_full(self, x):
        c = x.shape[-1]
        h, s = self.half, self.small
        cut = self.large_n * h * h
        large = x[:, :cut].reshape(2, 2, self.large_n, h, h, c).transpose(2, 3, 0, 4, 1, 5)
        small = x[:, cut:].reshape(2, 2, self.small_n, s, s, c).transpose(2, 3, 0, 4, 1, 5)
        large = large.reshape(self.large_n, 2 * h, 2 * h, c)
        small = small.reshape(self.small_n, 2 * s, 2 * s, c)
        pad = 2 * h - 2 * s
        return self.join(large, jnp.pad(small, ((0, 0), (0, pad), (0, pad), (0, 0))))


def strided_tap(tap):
    r, c = divmod(tap, 3)
    plane = 2 * int(r != 1) + int(c != 1)
    shift = 3 * (0 if r == 0 else 1) + (0 if c == 0 else 1)
    return plane, shift


def unit_tap(tap):
    return 0, tap


VMEM_LIMIT = 56 * 1024 * 1024
PARAMS = pltpu.CompilerParams(vmem_limit_bytes=VMEM_LIMIT)
WHOLE = pl.BlockSpec(memory_space=pltpu.VMEM)


def conv_forward(taps, act, shifts, weight):
    planes, rows, depth = act.shape
    width = weight.shape[2]

    def kernel(act_ref, shift_ref, weight_ref, out_ref, cols_ref):
        total = jnp.zeros((rows, width), F32)
        for tap in range(9):
            plane, shift = taps(tap)
            a = act_ref[plane]
            if shift != 4:
                a = jnp.dot(shift_ref[shift], a, preferred_element_type=F32).astype(BF16)
            cols_ref[tap] = a
            total = total + jnp.dot(a, weight_ref[tap], preferred_element_type=F32)
        out_ref[...] = total

    return pl.pallas_call(
        kernel,
        out_shape=(
            jax.ShapeDtypeStruct((rows, width), F32),
            jax.ShapeDtypeStruct((9, rows, depth), BF16),
        ),
        in_specs=[WHOLE] * 3,
        out_specs=(WHOLE, WHOLE),
        compiler_params=PARAMS,
    )(act, shifts, weight)


def conv_backward(taps, planes, grad, shifts, weight):
    rows = grad.shape[0]
    depth = weight.shape[1]

    def kernel(grad_ref, shift_ref, weight_ref, out_ref):
        for plane in range(planes):
            total = None
            for tap in range(9):
                at, shift = taps(tap)
                if at != plane:
                    continue
                g = grad_ref[...]
                if shift != 4:
                    g = jnp.dot(shift_ref[8 - shift], g, preferred_element_type=F32).astype(BF16)
                part = lax.dot_general(
                    g, weight_ref[tap], (((1,), (1,)), ((), ())), preferred_element_type=F32
                )
                total = part if total is None else total + part
            out_ref[plane] = total.astype(BF16)

    return pl.pallas_call(
        kernel,
        out_shape=jax.ShapeDtypeStruct((planes, rows, depth), BF16),
        in_specs=[WHOLE] * 3,
        out_specs=WHOLE,
        compiler_params=PARAMS,
    )(grad, shifts, weight)


def dot(a, b):
    return jnp.dot(a, b, preferred_element_type=F32)


def dot_nt(a, b):
    return lax.dot_general(a, b, (((1,), (1,)), ((), ())), preferred_element_type=F32)


def dot_tn(a, b):
    return lax.dot_general(a, b, (((0,), (0,)), ((), ())), preferred_element_type=F32)


def local(
    block_input,
    first_reduce,
    first_spatial,
    first_expand,
    first_shortcut,
    second_reduce,
    second_spatial,
    second_expand,
    first_mid_gain,
    first_mid_bias,
    first_wide_gain,
    first_wide_bias,
    second_mid_gain,
    second_mid_bias,
    second_wide_gain,
    second_wide_bias,
    subnet_widths,
    subnet_ids,
    crop_sides,
    cotangent,
):
    nb, nc = lax.axis_size("batch"), lax.axis_size("chan")
    spread = nb // nc
    crops, side = block_input.shape[0], block_input.shape[1]
    geo = Geometry(crops, side)
    px = geo.pixels
    subs = subnet_widths.shape[0]
    me = lax.axis_index("chan")
    mid = first_reduce.shape[1]
    wide = first_shortcut.shape[1]
    part_in = block_input.shape[3]

    def chan_swap(x, r):
        return lax.ppermute(x, "chan", [(i, i ^ r) for i in range(nc)])

    def gather_chan(x, axis=1):
        size = x.shape[axis]
        shape = list(x.shape)
        shape[axis] = size * nc
        out = jnp.zeros(shape, x.dtype)
        for r in range(nc):
            piece = x if r == 0 else chan_swap(x, r)
            out = lax.dynamic_update_slice_in_dim(out, piece, (me ^ r) * size, axis)
        return out

    def scatter_chan(x, axis=1):
        size = x.shape[axis] // nc
        total = None
        for r in range(nc):
            piece = lax.dynamic_slice_in_dim(x, (me ^ r) * size, size, axis)
            if r:
                piece = chan_swap(piece, r)
            piece = piece.astype(F32)
            total = piece if total is None else total + piece
        return total

    def sum_batch(x):
        y = lax.all_to_all(jnp.broadcast_to(x[None], (nb,) + x.shape), "batch", 0, 0, tiled=True)
        return jnp.sum(y, axis=0)

    turn = []
    for zc in range(nc):
        for j in range(spread):
            for c in range(nc):
                turn.append(((zc * spread + j) * nc + c, (c * spread + j) * nc + zc))

    def turn_share(x):
        return lax.ppermute(x, ALL, turn)

    start = lax.axis_index("batch") * crops
    sides = lax.dynamic_slice_in_dim(crop_sides, start, crops)
    ids = lax.dynamic_slice_in_dim(subnet_ids, start, crops)
    labels = jnp.arange(subs, dtype=jnp.int32)
    member_all = (subnet_ids[None, :] == labels[:, None]).astype(F32)
    halves = crop_sides // 2
    count_full = jnp.sum(member_all * (crop_sides * crop_sides).astype(F32)[None, :], axis=1)
    count_half = jnp.sum(member_all * (halves * halves).astype(F32)[None, :], axis=1)
    pick = jnp.asarray(geo.rows[:, 0:1] == np.arange(crops)[None, :])
    side_row = jnp.sum(jnp.where(pick, sides[None, :], 0), axis=1)
    id_row = jnp.sum(jnp.where(pick, ids[None, :], 0), axis=1)
    row_i, row_j = geo.rows[:, 1], geo.rows[:, 2]
    inside_half = (row_i < side_row // 2) & (row_j < side_row // 2)
    own = id_row[:, None] == labels[None, :]
    seg_half = (own & inside_half[:, None]).astype(F32)
    planes = []
    for p in range(2):
        for q in range(2):
            inside = (2 * row_i + p < side_row) & (2 * row_j + q < side_row)
            planes.append((own & inside[:, None]).astype(F32))
    seg_full = jnp.concatenate(planes, axis=0)
    mask_half = jnp.sum(seg_half, axis=1, keepdims=True)
    mask_full = jnp.sum(seg_full, axis=1, keepdims=True)
    channel = (me * mid + jnp.arange(mid, dtype=jnp.int32))[None, :]
    active = (channel < subnet_widths[:, None]).astype(F32)

    def select(seg, table):
        total = seg[:, 0:1] * table[0:1]
        for s in range(1, subs):
            total = total + seg[:, s : s + 1] * table[s : s + 1]
        return total

    def sums(seg, *fields):
        return jnp.concatenate(
            [jnp.sum(f * seg[:, s : s + 1], axis=0, keepdims=True) for f in fields for s in range(subs)],
            axis=0,
        )

    def forward_tables(totals, counts):
        average = totals[:subs] / counts[:, None]
        squares = totals[subs:] / counts[:, None]
        return average, lax.rsqrt(squares - average * average + EPS)

    def normed(v, seg, average, inverse):
        return (v - select(seg, average)) * select(seg, inverse)

    def norm_grad(u, xhat, seg, inverse, gain, gsum, xsum, counts):
        scale = select(seg, gain[None, :] * inverse)
        return scale * (
            u - (select(seg, gsum / counts[:, None]) + xhat * select(seg, xsum / counts[:, None]))
        )

    rows128 = lambda w: jnp.concatenate([w[:, k : k + mid] for k in range(0, w.shape[1], mid)], axis=0)
    r1, s1, e1, sc, r2, s2, e2 = (
        w.astype(BF16)
        for w in (first_reduce, first_spatial, first_expand, first_shortcut, second_reduce, second_spatial, second_expand)
    )
    s_rows = s1.shape[2]
    e_cols = e1.shape[1]

    def gather_batch(x):
        return lax.all_gather(x, "batch", axis=0, tiled=False)

    group_a = gather_batch(jnp.concatenate([r1, s1.reshape(9 * s_rows, mid)], axis=0))
    r1_w = group_a[:, : r1.shape[0]].reshape(-1, mid)
    s1_w = group_a[:, r1.shape[0] :].reshape(nb, 9, s_rows, mid).transpose(1, 0, 2, 3).reshape(9, nb * s_rows, mid)
    turned = turn_share(
        jnp.concatenate([jnp.swapaxes(e1, 0, 1), r2, jnp.swapaxes(e2, 0, 1)], axis=0)
    )
    t_e1, t_r2, t_e2 = turned[:e_cols], turned[e_cols : e_cols + r2.shape[0]], turned[e_cols + r2.shape[0] :]
    group_b = gather_batch(jnp.concatenate([t_e1, t_r2, rows128(sc)], axis=0))
    group_c = gather_batch(jnp.concatenate([s2.reshape(9 * s_rows, mid), t_e2], axis=0))

    def expand_weight(x):
        return x.reshape(nc, spread, e_cols, mid).transpose(1, 2, 0, 3).reshape(spread * e_cols, nc * mid)

    e1_t = expand_weight(group_b[:, :e_cols])
    r2_w = group_b[:, e_cols : e_cols + r2.shape[0]].reshape(nc, wide, mid).transpose(1, 0, 2).reshape(wide, nc * mid)
    sc_part = group_b[:, e_cols + r2.shape[0] :]
    sc_w = sc_part.reshape(nb, wide // mid, -1, mid).transpose(0, 2, 1, 3).reshape(-1, wide)
    s2_w = group_c[:, : 9 * s_rows].reshape(nb, 9, s_rows, mid).transpose(1, 0, 2, 3).reshape(9, nb * s_rows, mid)
    e2_t = expand_weight(group_c[:, 9 * s_rows :])

    shifts = jnp.asarray(geo.shifts, BF16)

    entry = geo.pack_full(block_input).reshape(4 * px, part_in)
    entry = jnp.where(mask_full > 0, entry, jnp.zeros_like(entry))
    whole_entry = gather_chan(entry)
    pre_one = dot(whole_entry, r1_w)
    avg_one, inv_one = forward_tables(sum_batch(sums(seg_full, pre_one, pre_one * pre_one)), count_full)
    xhat_one = normed(pre_one, seg_full, avg_one, inv_one)
    norm_one = first_mid_gain[0] * xhat_one + first_mid_bias[0]
    keep_full = select(seg_full, active)
    act_one = (jax.nn.silu(norm_one) * keep_full).astype(BF16)
    slope_one = silu_slope(norm_one) * keep_full
    whole_one = gather_chan(act_one).reshape(4, px, -1)
    pre_two, cols_one = conv_forward(strided_tap, whole_one, shifts, s1_w)

    short_in = whole_entry[:px]
    pre_short = dot(short_in, sc_w)

    keep_half = select(seg_half, active)

    def mid_forward(pre, gain, bias):
        avg, inv = forward_tables(sum_batch(sums(seg_half, pre, pre * pre)), count_half)
        xhat = normed(pre, seg_half, avg, inv)
        norm = gain * xhat + bias
        act = (jax.nn.silu(norm) * keep_half).astype(BF16)
        return act, xhat, inv, silu_slope(norm) * keep_half

    act_two, xhat_two, inv_two, slope_two = mid_forward(pre_two, first_mid_gain[1], first_mid_bias[1])
    whole_two = gather_chan(act_two)
    pre_three = dot_nt(whole_two, e1_t)
    tot_wide = sum_batch(
        sums(seg_half, pre_three, pre_three * pre_three, pre_short, pre_short * pre_short)
    )
    avg_three, inv_three = forward_tables(tot_wide[: 2 * subs], count_half)
    avg_short, inv_short = forward_tables(tot_wide[2 * subs :], count_half)
    xhat_three = normed(pre_three, seg_half, avg_three, inv_three)
    xhat_short = normed(pre_short, seg_half, avg_short, inv_short)
    sum_one = (
        first_wide_gain[0] * xhat_three
        + first_wide_bias[0]
        + first_wide_gain[1] * xhat_short
        + first_wide_bias[1]
    )
    section_out = jax.nn.silu(sum_one) * mask_half
    slope_section = silu_slope(sum_one) * mask_half
    section_low = section_out.astype(BF16)

    pre_four = scatter_chan(dot(section_low, r2_w).astype(BF16))
    act_four, xhat_four, inv_four, slope_four = mid_forward(pre_four, second_mid_gain[0], second_mid_bias[0])
    pre_five, cols_four = conv_forward(unit_tap, gather_chan(act_four)[None], shifts, s2_w)
    act_five, xhat_five, inv_five, slope_five = mid_forward(pre_five, second_mid_gain[1], second_mid_bias[1])
    whole_five = gather_chan(act_five)
    pre_six = dot_nt(whole_five, e2_t)
    avg_six, inv_six = forward_tables(sum_batch(sums(seg_half, pre_six, pre_six * pre_six)), count_half)
    xhat_six = normed(pre_six, seg_half, avg_six, inv_six)
    sum_two = second_wide_gain * xhat_six + second_wide_bias + section_out
    output = geo.unpack_half(jax.nn.silu(sum_two) * mask_half)

    grad_final = geo.pack_half(cotangent).astype(F32) * mask_half * silu_slope(sum_two)

    def backward(u, xhat, seg, inv, gain, counts):
        totals = sum_batch(sums(seg, u, u * xhat))
        gsum, xsum = totals[:subs], totals[subs:]
        grad = norm_grad(u, xhat, seg, inv, gain, gsum, xsum, counts).astype(BF16)
        return grad, jnp.sum(xsum, axis=0), jnp.sum(gsum, axis=0)

    grad_six, wide_two_gain, wide_two_bias = backward(
        grad_final, xhat_six, seg_half, inv_six, second_wide_gain, count_half
    )
    u_five = scatter_chan(dot(grad_six, e2_t).astype(BF16)) * slope_five
    e2_grad = dot_tn(grad_six, whole_five).astype(BF16)
    grad_five, mid_five_gain, mid_five_bias = backward(
        u_five, xhat_five, seg_half, inv_five, second_mid_gain[1], count_half
    )
    back_four = scatter_chan(conv_backward(unit_tap, 1, grad_five, shifts, s2_w)[0])
    s2_grad = lax.dot_general(
        cols_four, grad_five, (((1,), (0,)), ((), ())), preferred_element_type=F32
    ).astype(BF16)
    grad_four, mid_four_gain, mid_four_bias = backward(
        back_four * slope_four, xhat_four, seg_half, inv_four, second_mid_gain[0], count_half
    )
    whole_grad_four = gather_chan(grad_four)
    back_section = dot_nt(whole_grad_four, r2_w) + grad_final
    r2_grad = dot_tn(section_low, whole_grad_four).astype(BF16)

    u_wide = back_section * slope_section
    tot_back = sum_batch(sums(seg_half, u_wide, u_wide * xhat_three, u_wide * xhat_short))
    gsum_wide, xsum_three, xsum_short = tot_back[:subs], tot_back[subs : 2 * subs], tot_back[2 * subs :]
    grad_three = norm_grad(
        u_wide, xhat_three, seg_half, inv_three, first_wide_gain[0], gsum_wide, xsum_three, count_half
    ).astype(BF16)
    grad_short = norm_grad(
        u_wide, xhat_short, seg_half, inv_short, first_wide_gain[1], gsum_wide, xsum_short, count_half
    ).astype(BF16)
    wide_one_bias = jnp.sum(gsum_wide, axis=0)
    back_two = scatter_chan(dot(grad_three, e1_t).astype(BF16))
    e1_grad = dot_tn(grad_three, whole_two).astype(BF16)
    sc_grad = dot_tn(short_in, grad_short).astype(BF16)
    from_short = dot_nt(grad_short, sc_w)
    grad_two, mid_two_gain, mid_two_bias = backward(
        back_two * slope_two, xhat_two, seg_half, inv_two, first_mid_gain[1], count_half
    )
    back_one = scatter_chan(
        conv_backward(strided_tap, 4, grad_two, shifts, s1_w).reshape(4 * px, nc * mid)
    )
    s1_grad = lax.dot_general(
        cols_one, grad_two, (((1,), (0,)), ((), ())), preferred_element_type=F32
    ).astype(BF16)
    grad_one, mid_one_gain, mid_one_bias = backward(
        back_one * slope_one, xhat_one, seg_full, inv_one, first_mid_gain[0], count_full
    )
    r1_grad = dot_tn(whole_entry, grad_one).astype(BF16)
    from_reduce = dot_nt(grad_one, r1_w)
    from_reduce = jnp.concatenate([from_reduce[:px] + from_short, from_reduce[px:]], axis=0)
    input_grad = geo.unpack_full(
        (scatter_chan(from_reduce.astype(BF16)) * mask_full).reshape(4, px, part_in)
    )

    def to_owners(*parts):
        cat = jnp.concatenate(parts, axis=1)
        out = lax.psum_scatter(cat, "batch", scatter_dimension=0, tiled=False)
        cuts = np.cumsum([p.shape[1] for p in parts])[:-1]
        return jnp.split(out, cuts, axis=0)

    def expand_shares(g):
        return g.reshape(spread, e_cols, nc, mid).transpose(2, 0, 1, 3).reshape(nb, e_cols, mid)

    def spatial_shares(g):
        return g.reshape(9, nb, s_rows, mid).transpose(1, 0, 2, 3).reshape(nb, 9 * s_rows, mid)

    r2_shares = r2_grad.reshape(wide, nc, mid).transpose(1, 0, 2).reshape(nb, wide // spread, mid)
    sc_shares = sc_grad.reshape(nb, -1, wide // mid, mid).transpose(0, 2, 1, 3).reshape(nb, -1, mid)
    e2_out, s2_out, r2_out = to_owners(expand_shares(e2_grad), spatial_shares(s2_grad), r2_shares)
    e1_out, sc_out = to_owners(expand_shares(e1_grad), sc_shares)
    s1_out, r1_out = to_owners(spatial_shares(s1_grad), r1_grad.reshape(nb, -1, mid))
    back = turn_share(jnp.concatenate([e1_out, r2_out, e2_out], axis=0)).astype(F32)
    e1_own, r2_own, e2_own = jnp.split(back, [e_cols, e_cols + r2.shape[0]], axis=0)
    sc_own = sc_out.astype(F32).reshape(wide // mid, -1, mid).transpose(1, 0, 2).reshape(-1, wide)
    return (
        output,
        input_grad,
        r1_out.astype(F32),
        s1_out.astype(F32).reshape(3, 3, s_rows, mid),
        e1_own.T,
        sc_own,
        r2_own,
        s2_out.astype(F32).reshape(3, 3, s_rows, mid),
        e2_own.T,
        jnp.stack([mid_one_gain, mid_two_gain]),
        jnp.stack([mid_one_bias, mid_two_bias]),
        jnp.stack([jnp.sum(xsum_three, axis=0), jnp.sum(xsum_short, axis=0)]),
        jnp.stack([wide_one_bias, wide_one_bias]),
        jnp.stack([mid_four_gain, mid_five_gain]),
        jnp.stack([mid_four_bias, mid_five_bias]),
        wide_two_gain,
        wide_two_bias,
    )


def solution(mesh):
    placed = (
        P("batch", None, None, "chan"),
        P("batch", "chan"),
        P(None, None, "batch", "chan"),
        P("chan", "batch"),
        P("batch", "chan"),
        P("batch", "chan"),
        P(None, None, "batch", "chan"),
        P("chan", "batch"),
        P(None, "chan"),
        P(None, "chan"),
        P(None, "chan"),
        P(None, "chan"),
        P(None, "chan"),
        P(None, "chan"),
        P("chan"),
        P("chan"),
        P(),
        P(),
        P(),
        P("batch", None, None, "chan"),
    )
    outs = (
        P("batch", None, None, "chan"),
        P("batch", None, None, "chan"),
        P("batch", "chan"),
        P(None, None, "batch", "chan"),
        P("chan", "batch"),
        P("batch", "chan"),
        P("batch", "chan"),
        P(None, None, "batch", "chan"),
        P("chan", "batch"),
        P(None, "chan"),
        P(None, "chan"),
        P(None, "chan"),
        P(None, "chan"),
        P(None, "chan"),
        P(None, "chan"),
        P("chan"),
        P("chan"),
    )
    return jax.shard_map(local, mesh=mesh, in_specs=placed, out_specs=outs, check_vma=False)
```

time: 1470 us -> 602 us (0.41)
  blocking collectives: 495 us -> 19.6 us
  waiting for transfers between devices: 580 us -> 292 us
  local copies, waits for them, and re-layouts: 196 us -> 77.5 us
  matrix products: 105 us -> 28.9 us
  starting transfers between devices: 21.4 us -> 78.1 us
  Pallas kernels: 0 us -> 21.4 us
    reduce_scatter x8 -> x3, waiting for transfers between devices: 494 us -> 91.9 us  [to_owners(): out = lax.psum_scatter(cat, 'batch', scatter_dimension=0, tiled=False)]
    psum x12 -> x0, blocking collectives: 285 us -> none  [the longest x6 144 us: norm_forward(): first_total, second_total = lax.psum((first_local, second_local), 'batch')]
    all_gather x10 -> x0, blocking collectives: 179 us -> none  [the longest x1 34.2 us: local(): lax.all_gather(second_reduce.astype(jnp.bfloat16), 'batch', axis=0, tiled...]
    ppermute x0 -> x38, waiting for transfers between devices: none -> 103 us  [the longest x36 82.7 us: chan_swap(): return lax.ppermute(x, 'chan', [(i, i ^ r) for i in range(nc)])]
    dot_general x69 -> x17, matrix products: 105 us -> 28.9 us  [the longest x5 8.95 us: dot_tn(): lax.dot_general(a, b, (((0,), (0,)), ((), ())), preferred_element_type=F32)]
    pad x4 -> x2, local copies, waits for them, and re-layouts: 68.7 us -> 0.5 us  [the longest x1 0.34 us: unpack_full(): jnp.pad(small, ((0, 0), (0, pad), (0, pad), (0, 0)))]
    slice x7 -> x38, local copies, waits for them, and re-layouts: 66.5 us -> 10.9 us  [the longest x1 1.35 us: local(): group_c[:, :9 * s_rows].reshape(nb, 9, s_rows, mid).transpose(1, 0, 2, 3)]
    all_to_all x4 -> x10, waiting for transfers between devices: 26.5 us -> 62.5 us  [sum_batch(): lax.all_to_all(jnp.broadcast_to(x[None], (nb,) + x.shape), 'batch', 0, 0,...]
  transfers between devices with their start and end apart: 20 -> 54, of which waited for: 13 -> 36; matrix products, arithmetic and copies ran while one was open for 9% -> 18% of each run, Pallas kernels for 0% -> 2%
where the time goes in v1:
time: 602 us; the launch traced here: 593 us
  waiting for transfers between devices  292 us (49%)
  starting transfers between devices  78.1 us (13%)
  local copies, waits for them, and re-layouts  77.5 us (13%)
  other arithmetic  57.1 us (9%)
  matrix products  28.9 us (5%)
  Pallas kernels  21.4 us (4%)
  blocking collectives  19.6 us (3%)
  between operations  17.7 us (3%)
    reduce_scatter x3, waiting for transfers between devices, to_owners(): out = lax.psum_scatter(cat, 'batch', scatter_dimension=0, tiled=False)  91.9 us
    ppermute x36, waiting for transfers between devices, chan_swap(): return lax.ppermute(x, 'chan', [(i, i ^ r) for i in range(nc)])  82.7 us
    all_to_all x10, waiting for transfers between devices, sum_batch(): lax.all_to_all(jnp.broadcast_to(x[None], (nb,) + x.shape), 'batch', 0, 0,...  62.5 us
    all_to_all x10, starting transfers between devices, sum_batch(): lax.all_to_all(jnp.broadcast_to(x[None], (nb,) + x.shape), 'batch', 0, 0,...  48.2 us
    all_gather x3, waiting for transfers between devices, gather_batch(): return lax.all_gather(x, 'batch', axis=0, tiled=False)  35.3 us
    ppermute x36, starting transfers between devices, chan_swap(): return lax.ppermute(x, 'chan', [(i, i ^ r) for i in range(nc)])  21.7 us
    ppermute x2, waiting for transfers between devices, turn_share(): return lax.ppermute(x, ALL, turn)  20 us
    all_to_all x2, blocking collectives, sum_batch(): lax.all_to_all(jnp.broadcast_to(x[None], (nb,) + x.shape), 'batch', 0, 0,...  19.6 us
  transfers between devices with their start and end apart: 54, of which 36 were waited for; matrix products, arithmetic and copies ran while one was open for 18% of the time, Pallas kernels for 2%

profile of v1, /device:TPU:4, one launch (start us, length us, event | category | flops | bytes accessed | tf_op | source)
XLA Modules:
  0.0 592.7 jit_solution(4498560102191630724)
XLA Ops:
  7.2 2.0 copy.158
  14.6 1.9 collective-permute-start.2
  19.9 4.4 collective-permute-start.9
  28.4 12.6 %collective-permute-done.9 = bf16[768,128]{0,1:T(8,128)(2,1)} collective-permute-done((bf16[768,128]{0,1:T(8,128)(2,1)}, bf16[768,128]{0,1:T(8,128)(2,1)}, u32[]{:S(2)}, u32[]{:S(2)}) %collective-permute-start.9) | collective-permute-done | bytes 196640 | tf_op jit(solution)/shard_map/ppermute | solution.py:245
  45.1 3.3 collective-permute-done.2
  48.5 17.3 %all-gather.7.cloned.1.call-done = bf16[5632,128]{1,0:T(8,128)(2,1)} async-done(((bf16[704,128]{1,0:T(8,128)(2,1)}), bf16[5632,128]{1,0:T(8,128)(2,1)}) %all-gather.7.cloned.1.call-update) | async-done | bytes 1441808 | tf_op jit(solution)/shard_map/all_gather | solution.py:308
  69.1 3.3 all-to-all-start
  72.7 6.6 %all-to-all-done = f32[8,6,128]{2,1,0:T(8,128)S(1)} async-done(((f32[8,6,128]{2,1,0:T(8,128)}), f32[8,6,128]{2,1,0:T(8,128)S(1)}, u32[]{:S(2)}, u32[]{:S(2)}) %all-to-all-start) | async-done | bytes 24608 | tf_op jit(solution)/shard_map/all_to_all | solution.py:235
  80.1 2.8 constant_dynamic-update-slice_fusion.15
  87.1 6.2 %collective-permute-done.4 = bf16[1216,128]{1,0:T(8,128)(2,1)S(1)} collective-permute-done((bf16[1216,128]{1,0:T(8,128)(2,1)}, bf16[1216,128]{1,0:T(8,128)(2,1)S(1)}, u32[]{:S(2)}, u32[]{:S(2)}) %collective-permute-start.4) | collective-permute-done | bytes 311328 | tf_op jit(solution)/shard_map/ppermute | solution.py:211
  93.3 5.8 collective-permute-done.5
  100.3 6.0 %shard_map.431 = (f32[304,128]{1,0:T(8,128)}, bf16[9,304,512]{2,1,0:T(8,128)(2,1)}) custom-call(bf16[4,304,512]{2,1,0:T(8,128)(2,1)} %bitcast.469, bf16[9,304,304]{2,1,0:T(8,128)(2,1)} %constant.107.clone.shift_ref, bf16[9,512,128]{2,1,0:T(8,128)(2,1)} %bitcast.458), custom_call_target="tpu_custom_call" | custom-call | tf_op jit(solution)/shard_map/pallas_call | solution.py:124
  107.4 9.6 %all_to_all.60 = f32[8,6,128]{2,1,0:T(8,128)S(1)} all-to-all(f32[8,6,128]{2,1,0:T(8,128)S(1)} %broadcast_in_dim.430), channel_id=1, replica_groups=mesh['batch'=8,'chan'=4] {'batch'}, dimensions={0} | all-to-all | bytes 49152 | tf_op jit(solution)/shard_map/all_to_all | solution.py:235
  121.0 3.3 collective-permute-done.7
  125.9 3.2 copy.168
  132.8 2.0 fusion.3
  137.6 3.4 all-to-all-start.2
  143.7 6.9 %all-to-all-done.2 = f32[8,12,512]{2,1,0:T(8,128)S(1)} async-done(((f32[8,12,512]{2,1,0:T(8,128)}), f32[8,12,512]{2,1,0:T(8,128)S(1)}, u32[]{:S(2)}, u32[]{:S(2)}) %all-to-all-start.2) | async-done | bytes 196640 | tf_op jit(solution)/shard_map/all_to_all | solution.py:235
  151.4 2.5 multiply_multiply_fusion.3
  156.4 3.3 collective-permute-done.11
  161.4 3.6 all-to-all-start.3
  165.0 6.6 %all-to-all-done.3 = f32[8,6,128]{2,1,0:T(8,128)S(1)} async-done(((f32[8,6,128]{2,1,0:T(8,128)}), f32[8,6,128]{2,1,0:T(8,128)S(1)}, u32[]{:S(2)}, u32[]{:S(2)}) %all-to-all-start.3) | async-done | bytes 24608 | tf_op jit(solution)/shard_map/all_to_all | solution.py:235
  173.2 18.0 %all-gather.11.cloned.1.call-done = bf16[6656,128]{1,0:T(8,128)(2,1)} async-done(((bf16[832,128]{1,0:T(8,128)(2,1)}), bf16[6656,128]{1,0:T(8,128)(2,1)}) %all-gather.11.cloned.1.call-update) | async-done | bytes 1703952 | tf_op jit(solution)/shard_map/all_gather | solution.py:308
  194.3 4.6 collective-permute-done.14
  199.7 5.8 shard_map.432
  206.7 10.0 %all_to_all.61 = f32[8,6,128]{2,1,0:T(8,128)S(1)} all-to-all(f32[8,6,128]{2,1,0:T(8,128)S(1)} %broadcast_in_dim.461), channel_id=1, replica_groups=mesh['batch'=8,'chan'=4] {'batch'}, dimensions={0} | all-to-all | bytes 49152 | tf_op jit(solution)/shard_map/all_to_all | solution.py:235
  222.1 3.3 collective-permute-done.17
  228.4 16.3 %all-to-all-start.5 = ((f32[8,6,512]{2,1,0:T(8,128)}), f32[8,6,512]{2,1,0:T(8,128)}, u32[]{:S(2)}, u32[]{:S(2)}) async-start(f32[8,6,512]{2,1,0:T(8,128)} %broadcast_in_dim.468), calls=%async_computation.5 | async-start | bytes 262144 | tf_op jit(solution)/shard_map/all_to_all | solution.py:235
  247.0 5.1 all-to-all-done.5
  253.2 2.3 multiply_reduce_fusion.15
  256.2 4.0 all-to-all-start.6
  260.2 7.3 %all-to-all-done.6 = f32[8,6,512]{2,1,0:T(8,128)} async-done(((f32[8,6,512]{2,1,0:T(8,128)}), f32[8,6,512]{2,1,0:T(8,128)}, u32[]{:S(2)}, u32[]{:S(2)}) %all-to-all-start.6) | async-done | bytes 98336 | tf_op jit(solution)/shard_map/all_to_all | solution.py:235
  273.0 3.3 collective-permute-done.20
  278.1 3.3 all-to-all-start.7
  281.5 6.6 %all-to-all-done.7 = f32[8,6,128]{2,1,0:T(8,128)S(1)} async-done(((f32[8,6,128]{2,1,0:T(8,128)}), f32[8,6,128]{2,1,0:T(8,128)S(1)}, u32[]{:S(2)}, u32[]{:S(2)}) %all-to-all-start.7) | async-done | bytes 24608 | tf_op jit(solution)/shard_map/all_to_all | solution.py:235
  289.5 5.1 shard_map.433
  297.6 3.4 collective-permute-done.23
  304.7 4.0 all-to-all-start.8
  309.2 6.2 %all-to-all-done.8 = f32[8,6,128]{2,1,0:T(8,128)} async-done(((f32[8,6,128]{2,1,0:T(8,128)}), f32[8,6,128]{2,1,0:T(8,128)}, u32[]{:S(2)}, u32[]{:S(2)}) %all-to-all-start.8) | async-done | bytes 24608 | tf_op jit(solution)/shard_map/all_to_all | solution.py:235
  321.0 3.3 collective-permute-done.26
  325.2 3.2 multiply_reduce_fusion.9
  329.2 3.4 all-to-all-start.9
  332.8 9.4 %all-to-all-done.9 = f32[8,9,512]{2,1,0:T(8,128)S(1)} async-done(((f32[8,9,512]{2,1,0:T(8,128)}), f32[8,9,512]{2,1,0:T(8,128)S(1)}, u32[]{:S(2)}, u32[]{:S(2)}) %all-to-all-start.9) | async-done | bytes 147488 | tf_op jit(solution)/shard_map/all_to_all | solution.py:235
  348.6 2.6 convolution_convert_fusion.2
  356.3 3.6 all-to-all-start.10
  361.2 5.3 all-to-all-done.10
  367.9 4.5 shard_map.434
  375.8 8.3 %collective-permute-done.32 = bf16[1216,128]{1,0:T(8,128)(2,1)S(1)} collective-permute-done((bf16[1216,128]{1,0:T(8,128)(2,1)S(1)}, bf16[1216,128]{1,0:T(8,128)(2,1)S(1)}, u32[]{:S(2)}, u32[]{:S(2)}) %collective-permute-start.32) | collective-permute-done | bytes 311328 | tf_op jit(solution)/shard_map/ppermute | solution.py:211
  384.1 5.8 collective-permute-done.33
  389.9 2.0 multiply_reduce_fusion
  392.5 3.3 all-to-all-start.11
  395.9 3.0 convolution_convert_fusion.1
  400.0 2.4 all-to-all-done.11
  403.1 3.3 convolution_convert_fusion.9
  409.5 3.0 convolution_convert_fusion
  416.2 2.7 pad_maximum_fusion.1
  434.5 11.5 %collective-permute-done.35 = bf16[1216,256]{1,0:T(8,128)(2,1)S(1)} collective-permute-done((bf16[1216,256]{1,0:T(8,128)(2,1)S(1)}, bf16[1216,256]{1,0:T(8,128)(2,1)S(1)}, u32[]{:S(2)}, u32[]{:S(2)}) %collective-permute-start.35) | collective-permute-done | bytes 622624 | tf_op jit(solution)/shard_map/ppermute | solution.py:211
  446.1 12.4 %collective-permute-done.36 = bf16[1216,256]{1,0:T(8,128)(2,1)S(1)} collective-permute-done((bf16[1216,256]{1,0:T(8,128)(2,1)S(1)}, bf16[1216,256]{1,0:T(8,128)(2,1)S(1)}, u32[]{:S(2)}, u32[]{:S(2)}) %collective-permute-start.36) | collective-permute-done | bytes 622624 | tf_op jit(solution)/shard_map/ppermute | solution.py:211
  461.3 2.2 reshape.329
  468.5 4.1 copy.201
  475.1 22.5 %reduce-scatter.4.cloned.1.call-done = bf16[1,704,128]{2,1,0:T(8,128)(2,1)} async-done(((bf16[8,704,128]{2,1,0:T(8,128)(2,1)}), bf16[1,704,128]{2,1,0:T(8,128)(2,1)}) %reduce-scatter.4.cloned.1.call-update) | async-done | bytes 180240 | tf_op jit(solution)/shard_map/reduce_scatter | solution.py:450
  499.2 69.4 %reduce-scatter.8.cloned.1.call-done = bf16[1,1088,128]{2,1,0:T(8,128)(2,1)} async-done(((bf16[8,1088,128]{2,1,0:T(8,128)(2,1)}), bf16[1,1088,128]{2,1,0:T(8,128)(2,1)}) %reduce-scatter.8.cloned.1.call-update) | async-done | bytes 278544 | tf_op jit(solution)/shard_map/reduce_scatter | solution.py:450
  569.5 3.3 collective-permute-start.37
  575.9 7.3 %collective-permute-done.37 = bf16[768,128]{1,0:T(8,128)(2,1)S(1)} collective-permute-done((bf16[768,128]{1,0:T(8,128)(2,1)S(1)}, bf16[768,128]{1,0:T(8,128)(2,1)S(1)}, u32[]{:S(2)}, u32[]{:S(2)}) %collective-permute-start.37) | collective-permute-done | bytes 196640 | tf_op jit(solution)/shard_map/ppermute | solution.py:245
  (652 shorter events, 147.8 us)
Async XLA Ops:
  7.2 58.5 %all-gather.7.cloned.1.call-start = ((), (), s32[]{:S(2)}) async-start(), calls=%async_computation.18 | async-start | bytes 1622016 | tf_op jit(solution)/shard_map/all_gather | solution.py:308
  14.5 28.2 %collective-permute-start = (bf16[1216,256]{1,0:T(8,128)(2,1)}, bf16[1216,256]{1,0:T(8,128)(2,1)}, u32[]{:S(2)}, u32[]{:S(2)}) collective-permute-start(bf16[1216,256]{1,0:T(8,128)(2,1)} %get-tuple-element.485), channel_id=1, source_target_pairs={{0,1},{1,0},{2,3},{3,2},{4,5},{5,4},{6,7},{7,6},{8,9},{9,8},{10,11... | collective-permute-start | bytes 1867784 | tf_op jit(solution)/shard_map/ppermute | solution.py:211
  14.5 29.4 %collective-permute-start.1 = (bf16[1216,256]{1,0:T(8,128)(2,1)}, bf16[1216,256]{1,0:T(8,128)(2,1)}, u32[]{:S(2)}, u32[]{:S(2)}) collective-permute-start(bf16[1216,256]{1,0:T(8,128)(2,1)} %get-tuple-element.485), channel_id=1, source_target_pairs={{0,2},{1,3},{2,0},{3,1},{4,6},{5,7},{6,4},{7,5},{8,10},{9,11},{10,... | collective-permute-start | bytes 1867784 | tf_op jit(solution)/shard_map/ppermute | solution.py:211
  14.6 33.8 %collective-permute-start.2 = (bf16[1216,256]{1,0:T(8,128)(2,1)}, bf16[1216,256]{1,0:T(8,128)(2,1)S(1)}, u32[]{:S(2)}, u32[]{:S(2)}) collective-permute-start(bf16[1216,256]{1,0:T(8,128)(2,1)} %get-tuple-element.485), channel_id=1, source_target_pairs={{0,3},{1,2},{2,1},{3,0},{4,7},{5,6},{6,5},{7,4},{8,11},{9,10},{10,... | collective-permute-start | bytes 1867784 | tf_op jit(solution)/shard_map/ppermute | solution.py:211
  17.2 108.7 %all-gather.9.cloned.1.call-start = ((), (), s32[]{:S(2)}) async-start(), calls=%async_computation.19 | async-start | bytes 2359296 | tf_op jit(solution)/shard_map/all_gather | solution.py:308
  19.9 21.1 %collective-permute-start.9 = (bf16[768,128]{0,1:T(8,128)(2,1)}, bf16[768,128]{0,1:T(8,128)(2,1)}, u32[]{:S(2)}, u32[]{:S(2)}) collective-permute-start(bf16[768,128]{0,1:T(8,128)(2,1)} %pad_maximum_fusion.6), channel_id=1, source_target_pairs={{0,0},{1,8},{2,16},{3,24},{4,4},{5,12},{6,20},{7,28},{8,1},{9,9},{... | collective-permute-start | bytes 589832 | tf_op jit(solution)/shard_map/ppermute | solution.py:245
  27.2 52.8 %copy-start.40 = (f32[128]{0:T(128)}, f32[128]{0:T(128)S(1)}, u32[]{:S(2)}) copy-start(f32[128]{0:T(128)S(1)} %get-tuple-element.472) | copy-start | bytes 1540
  27.2 52.8 %copy-start.42 = (f32[128]{0:T(128)}, f32[128]{0:T(128)S(1)}, u32[]{:S(2)}) copy-start(f32[128]{0:T(128)S(1)} %get-tuple-element.473) | copy-start | bytes 1540
  69.1 10.1 %all-to-all-start = ((f32[8,6,128]{2,1,0:T(8,128)}), f32[8,6,128]{2,1,0:T(8,128)S(1)}, u32[]{:S(2)}, u32[]{:S(2)}) async-start(f32[8,6,128]{2,1,0:T(8,128)} %broadcast_in_dim.423), calls=%async_computation | async-start | bytes 65536 | tf_op jit(solution)/shard_map/all_to_all | solution.py:235
  82.9 3.1 collective-permute-start.3
  82.9 10.4 %collective-permute-start.4 = (bf16[1216,128]{1,0:T(8,128)(2,1)}, bf16[1216,128]{1,0:T(8,128)(2,1)S(1)}, u32[]{:S(2)}, u32[]{:S(2)}) collective-permute-start(bf16[1216,128]{1,0:T(8,128)(2,1)} %get-tuple-element.293), channel_id=1, source_target_pairs={{0,2},{1,3},{2,0},{3,1},{4,6},{5,7},{6,4},{7,5},{8,10},{9,11},{10,... | collective-permute-start | bytes 933896 | tf_op jit(solution)/shard_map/ppermute | solution.py:211
  84.7 14.5 %collective-permute-start.5 = (bf16[1216,128]{1,0:T(8,128)(2,1)}, bf16[1216,128]{1,0:T(8,128)(2,1)S(1)}, u32[]{:S(2)}, u32[]{:S(2)}) collective-permute-start(bf16[1216,128]{1,0:T(8,128)(2,1)} %get-tuple-element.293), channel_id=1, source_target_pairs={{0,3},{1,2},{2,1},{3,0},{4,7},{5,6},{6,5},{7,4},{8,11},{9,10},{10,... | collective-permute-start | bytes 933896 | tf_op jit(solution)/shard_map/ppermute | solution.py:211
  119.0 2.0 collective-permute-start.6
  119.1 32.3 %copy-start.48 = (f32[1,512]{1,0:T(1,128)}, f32[1,512]{1,0:T(1,128)S(1)}, u32[]{:S(2)}) copy-start(f32[1,512]{1,0:T(1,128)S(1)} %get-tuple-element.399) | copy-start | bytes 6148
  119.1 32.3 %copy-start.49 = (f32[1,512]{1,0:T(1,128)}, f32[1,512]{1,0:T(1,128)S(1)}, u32[]{:S(2)}) copy-start(f32[1,512]{1,0:T(1,128)S(1)} %get-tuple-element.400) | copy-start | bytes 6148
  119.1 5.2 collective-permute-start.7
  119.7 5.4 collective-permute-start.8
  137.6 13.0 %all-to-all-start.2 = ((f32[8,12,512]{2,1,0:T(8,128)}), f32[8,12,512]{2,1,0:T(8,128)S(1)}, u32[]{:S(2)}, u32[]{:S(2)}) async-start(f32[8,12,512]{2,1,0:T(8,128)} %broadcast_in_dim.443), calls=%async_computation.2 | async-start | bytes 524288 | tf_op jit(solution)/shard_map/all_to_all | solution.py:235
  141.0 50.2 %all-gather.11.cloned.1.call-start = ((), (), s32[]{:S(2)}) async-start(), calls=%async_computation.20 | async-start | bytes 1916928 | tf_op jit(solution)/shard_map/all_gather | solution.py:308
  154.4 2.0 collective-permute-start.10
  154.5 5.2 collective-permute-start.11
  155.1 5.4 collective-permute-start.12
  156.4 36.2 %copy-start.83 = (f32[128]{0:T(128)}, f32[128]{0:T(128)S(1)}, u32[]{:S(2)}) copy-start(f32[128]{0:T(128)S(1)} %get-tuple-element.474) | copy-start | bytes 1540
  161.4 10.2 %all-to-all-start.3 = ((f32[8,6,128]{2,1,0:T(8,128)}), f32[8,6,128]{2,1,0:T(8,128)S(1)}, u32[]{:S(2)}, u32[]{:S(2)}) async-start(f32[8,6,128]{2,1,0:T(8,128)} %broadcast_in_dim.450), calls=%async_computation.3 | async-start | bytes 65536 | tf_op jit(solution)/shard_map/all_to_all | solution.py:235
  164.9 28.8 %copy-start.97 = (f32[128]{0:T(128)}, f32[128]{0:T(128)S(1)}, u32[]{:S(2)}) copy-start(f32[128]{0:T(128)S(1)} %get-tuple-element.476) | copy-start | bytes 1540
  164.9 52.5 %copy-start.99 = (f32[128]{0:T(128)}, f32[128]{0:T(128)S(1)}, u32[]{:S(2)}) copy-start(f32[128]{0:T(128)S(1)} %get-tuple-element.477) | copy-start | bytes 1540
  173.2 21.1 %collective-permute-start.13 = (bf16[304,128]{1,0:T(8,128)(2,1)S(1)}, bf16[304,128]{1,0:T(8,128)(2,1)S(1)}, u32[]{:S(2)}, u32[]{:S(2)}) collective-permute-start(bf16[304,128]{1,0:T(8,128)(2,1)S(1)} %get-tuple-element.284), channel_id=1, source_target_pairs={{0,1},{1,0},{2,3},{3,2},{4,5},{5,4},{6,7},{7,6},{8,9},{9,8},{10,11... | collective-permute-start | bytes 233480 | tf_op jit(solution)/shard_map/ppermute | solution.py:211
  193.7 5.2 collective-permute-start.14
  194.3 4.7 collective-permute-start.15
  218.6 3.5 collective-permute-start.16
  220.2 5.3 collective-permute-start.17
  221.6 4.6 collective-permute-start.18
  228.4 23.8 %all-to-all-start.5 = ((f32[8,6,512]{2,1,0:T(8,128)}), f32[8,6,512]{2,1,0:T(8,128)}, u32[]{:S(2)}, u32[]{:S(2)}) async-start(f32[8,6,512]{2,1,0:T(8,128)} %broadcast_in_dim.468), calls=%async_computation.5 | async-start | bytes 262144 | tf_op jit(solution)/shard_map/all_to_all | solution.py:235
  256.2 11.4 %all-to-all-start.6 = ((f32[8,6,512]{2,1,0:T(8,128)}), f32[8,6,512]{2,1,0:T(8,128)}, u32[]{:S(2)}, u32[]{:S(2)}) async-start(f32[8,6,512]{2,1,0:T(8,128)} %broadcast_in_dim.475), calls=%async_computation.6 | async-start | bytes 262144 | tf_op jit(solution)/shard_map/all_to_all | solution.py:235
  271.1 1.9 collective-permute-start.19
  271.2 5.2 collective-permute-start.20
  272.6 4.6 collective-permute-start.21
  278.1 10.0 %all-to-all-start.7 = ((f32[8,6,128]{2,1,0:T(8,128)}), f32[8,6,128]{2,1,0:T(8,128)S(1)}, u32[]{:S(2)}, u32[]{:S(2)}) async-start(f32[8,6,128]{2,1,0:T(8,128)} %broadcast_in_dim.482), calls=%async_computation.7 | async-start | bytes 65536 | tf_op jit(solution)/shard_map/all_to_all | solution.py:235
  294.6 30.6 %copy-start.6 = (bf16[512,4,128]{0,2,1:T(8,128)(2,1)S(1)}, bf16[512,4,128]{0,2,1:T(8,128)(2,1)}, u32[]{:S(2)}) copy-start(bf16[512,4,128]{0,2,1:T(8,128)(2,1)} %copy-done.5) | copy-start | bytes 1572868
  295.6 1.9 collective-permute-start.22
  295.7 5.2 collective-permute-start.23
  297.1 4.6 collective-permute-start.24
  304.7 10.7 %all-to-all-start.8 = ((f32[8,6,128]{2,1,0:T(8,128)}), f32[8,6,128]{2,1,0:T(8,128)}, u32[]{:S(2)}, u32[]{:S(2)}) async-start(f32[8,6,128]{2,1,0:T(8,128)} %broadcast_in_dim.489), calls=%async_computation.8 | async-start | bytes 65536 | tf_op jit(solution)/shard_map/all_to_all | solution.py:235
  317.7 3.3 collective-permute-start.25
  319.1 5.2 collective-permute-start.26
  320.4 4.7 collective-permute-start.27
  329.2 12.9 %all-to-all-start.9 = ((f32[8,9,512]{2,1,0:T(8,128)}), f32[8,9,512]{2,1,0:T(8,128)S(1)}, u32[]{:S(2)}, u32[]{:S(2)}) async-start(f32[8,9,512]{2,1,0:T(8,128)} %broadcast_in_dim.499), calls=%async_computation.9 | async-start | bytes 524288 | tf_op jit(solution)/shard_map/all_to_all | solution.py:235
  346.6 7.8 %collective-permute-start.28 = (bf16[304,128]{1,0:T(8,128)(2,1)}, bf16[304,128]{1,0:T(8,128)(2,1)}, u32[]{:S(2)}, u32[]{:S(2)}) collective-permute-start(bf16[304,128]{1,0:T(8,128)(2,1)} %get-tuple-element.314), channel_id=1, source_target_pairs={{0,1},{1,0},{2,3},{3,2},{4,5},{5,4},{6,7},{7,6},{8,9},{9,8},{10,11... | collective-permute-start | bytes 233480 | tf_op jit(solution)/shard_map/ppermute | solution.py:211
  346.6 7.8 %collective-permute-start.29 = (bf16[304,128]{1,0:T(8,128)(2,1)}, bf16[304,128]{1,0:T(8,128)(2,1)}, u32[]{:S(2)}, u32[]{:S(2)}) collective-permute-start(bf16[304,128]{1,0:T(8,128)(2,1)} %get-tuple-element.316), channel_id=1, source_target_pairs={{0,2},{1,3},{2,0},{3,1},{4,6},{5,7},{6,4},{7,5},{8,10},{9,11},{10,... | collective-permute-start | bytes 233480 | tf_op jit(solution)/shard_map/ppermute | solution.py:211
  347.9 6.5 %collective-permute-start.30 = (bf16[304,128]{1,0:T(8,128)(2,1)}, bf16[304,128]{1,0:T(8,128)(2,1)}, u32[]{:S(2)}, u32[]{:S(2)}) collective-permute-start(bf16[304,128]{1,0:T(8,128)(2,1)} %get-tuple-element.315), channel_id=1, source_target_pairs={{0,3},{1,2},{2,1},{3,0},{4,7},{5,6},{6,5},{7,4},{8,11},{9,10},{10,... | collective-permute-start | bytes 233480 | tf_op jit(solution)/shard_map/ppermute | solution.py:211
  356.3 10.2 %all-to-all-start.10 = ((f32[8,6,128]{2,1,0:T(8,128)}), f32[8,6,128]{2,1,0:T(8,128)S(1)}, u32[]{:S(2)}, u32[]{:S(2)}) async-start(f32[8,6,128]{2,1,0:T(8,128)} %broadcast_in_dim.506), calls=%async_computation.10 | async-start | bytes 65536 | tf_op jit(solution)/shard_map/all_to_all | solution.py:235
  359.8 112.8 %reduce-scatter.6.cloned.1.call-start = ((), (), s32[]{:S(2)}) async-start(), calls=%async_computation.16 | async-start | bytes 1769472 | tf_op jit(solution)/shard_map/reduce_scatter | solution.py:450
  373.8 2.0 collective-permute-start.31
  373.9 10.2 %collective-permute-start.32 = (bf16[1216,128]{1,0:T(8,128)(2,1)S(1)}, bf16[1216,128]{1,0:T(8,128)(2,1)S(1)}, u32[]{:S(2)}, u32[]{:S(2)}) collective-permute-start(bf16[1216,128]{1,0:T(8,128)(2,1)S(1)} %get-tuple-element.309), channel_id=1, source_target_pairs={{0,2},{1,3},{2,0},{3,1},{4,6},{5,7},{6,4},{7,5},{8,10},{9,11},{10,... | collective-permute-start | bytes 933896 | tf_op jit(solution)/shard_map/ppermute | solution.py:211
  375.2 14.6 %collective-permute-start.33 = (bf16[1216,128]{1,0:T(8,128)(2,1)S(1)}, bf16[1216,128]{1,0:T(8,128)(2,1)S(1)}, u32[]{:S(2)}, u32[]{:S(2)}) collective-permute-start(bf16[1216,128]{1,0:T(8,128)(2,1)S(1)} %get-tuple-element.308), channel_id=1, source_target_pairs={{0,3},{1,2},{2,1},{3,0},{4,7},{5,6},{6,5},{7,4},{8,11},{9,10},{10,... | collective-permute-start | bytes 933896 | tf_op jit(solution)/shard_map/ppermute | solution.py:211
  375.7 27.3 %copy-start.110 = (f32[128]{0:T(128)}, f32[128]{0:T(128)S(1)}, u32[]{:S(2)}) copy-start(f32[128]{0:T(128)S(1)} %get-tuple-element.404) | copy-start | bytes 1540
  375.8 27.3 %copy-start.112 = (f32[128]{0:T(128)}, f32[128]{0:T(128)S(1)}, u32[]{:S(2)}) copy-start(f32[128]{0:T(128)S(1)} %get-tuple-element.405) | copy-start | bytes 1540
  392.5 10.0 %all-to-all-start.11 = ((f32[8,6,128]{2,1,0:T(8,128)}), f32[8,6,128]{2,1,0:T(8,128)S(1)}, u32[]{:S(2)}, u32[]{:S(2)}) async-start(f32[8,6,128]{2,1,0:T(8,128)} %broadcast_in_dim.513), calls=%async_computation.11 | async-start | bytes 65536 | tf_op jit(solution)/shard_map/all_to_all | solution.py:235
  395.8 101.7 %reduce-scatter.4.cloned.1.call-start = ((), (), s32[]{:S(2)}) async-start(), calls=%async_computation.15 | async-start | bytes 1622016 | tf_op jit(solution)/shard_map/reduce_scatter | solution.py:450
  407.7 160.9 %reduce-scatter.8.cloned.1.call-start = ((), (), s32[]{:S(2)}) async-start(), calls=%async_computation.17 | async-start | bytes 2506752 | tf_op jit(solution)/shard_map/reduce_scatter | solution.py:450
  429.1 5.5 collective-permute-start.34
  429.2 16.9 %collective-permute-start.35 = (bf16[1216,256]{1,0:T(8,128)(2,1)S(1)}, bf16[1216,256]{1,0:T(8,128)(2,1)S(1)}, u32[]{:S(2)}, u32[]{:S(2)}) collective-permute-start(bf16[1216,256]{1,0:T(8,128)(2,1)S(1)} %get-tuple-element.303), channel_id=1, source_target_pairs={{0,2},{1,3},{2,0},{3,1},{4,6},{5,7},{6,4},{7,5},{8,10},{9,11},{10,... | collective-permute-start | bytes 1867784 | tf_op jit(solution)/shard_map/ppermute | solution.py:211
  430.5 28.0 %collective-permute-start.36 = (bf16[1216,256]{1,0:T(8,128)(2,1)S(1)}, bf16[1216,256]{1,0:T(8,128)(2,1)S(1)}, u32[]{:S(2)}, u32[]{:S(2)}) collective-permute-start(bf16[1216,256]{1,0:T(8,128)(2,1)S(1)} %get-tuple-element.304), channel_id=1, source_target_pairs={{0,3},{1,2},{2,1},{3,0},{4,7},{5,6},{6,5},{7,4},{8,11},{9,10},{10,... | collective-permute-start | bytes 1867784 | tf_op jit(solution)/shard_map/ppermute | solution.py:211
  569.5 13.7 %collective-permute-start.37 = (bf16[768,128]{1,0:T(8,128)(2,1)S(1)}, bf16[768,128]{1,0:T(8,128)(2,1)S(1)}, u32[]{:S(2)}, u32[]{:S(2)}) collective-permute-start(bf16[768,128]{1,0:T(8,128)(2,1)S(1)} %pad_maximum_fusion.7), channel_id=1, source_target_pairs={{0,0},{1,8},{2,16},{3,24},{4,4},{5,12},{6,20},{7,28},{8,1},{9,9},{... | collective-permute-start | bytes 589832 | tf_op jit(solution)/shard_map/ppermute | solution.py:245
  (150 other events, 961.1 us)
Sparse Core Ops, SparseCore 0:
  17.3 48.4 all-gather.6
  68.5 48.1 all-gather.8
  144.6 46.5 all-gather.10
  363.8 66.2 reduce-scatter.5
  433.7 63.8 reduce-scatter.3
  501.3 67.2 reduce-scatter.7
